TPU v7x, 32 devices: a whole 2x2x4 slice. The times are simulated.
32 devices in a mesh: row: 8 (over y, x, core), col: 4 (over z).
Axes of the slice: x: 2, y: 2, z: 4, core: 2. Of those that a mesh axis runs over, the one named last changes fastest.
Arguments:
- features: bfloat16 [16384, 256], P('col', 'row'), may hold values from -6 to 6
- weight: bfloat16 [256, 256], replicated, may hold values from -0.375 to 0.375
- adj_values: bfloat16 [8, 4, 96, 128, 128], P('row', 'col'), may hold values from -0.125 to 0.125
- block_rows: int32 [8, 4, 96], P('row', 'col'), may hold values from 0 to 15, as said below
- block_cols: int32 [8, 4, 96], P('row', 'col'), may hold values from 0 to 31
- block_counts: int32 [8, 4], P('row', 'col'), may hold values from 1 to 96, as said below
- cotangent: bfloat16 [16384, 256], P(('row', 'col')), may hold values from -6 to 6
Outputs:
- output: bfloat16 [16384, 256], P(('row', 'col'))
- grad_weight: float32 [256, 256], replicated
- grad_features: bfloat16 [16384, 256], P('col', 'row')
Inputs may be any that keep to these rules, and one draw needn't show every extreme that they name: Within one tile the pairs (block_rows, block_cols) over all 96 slots are distinct. `block_counts`: some tile holds exactly 96 live blocks and some other tile exactly one in every draw.
All inputs are finite; a program needn't handle non-finite values.
Results may differ from a plain program's by a relative error of at most 0.029.
Values may be sent and summed in bfloat16 or wider, within the bound.
No kernel may reach another device: no remote copies, remote signals or barrier semaphores. Data moves between devices by JAX's collectives and lax.ppermute only.
A program may use at most 64 MiB of HBM per device.

v0:
```python
import functools
import math

import jax
import jax.numpy as jnp
from jax import lax
from jax.experimental import pallas as pl
from jax.experimental.pallas import tpu as pltpu
from jax.sharding import PartitionSpec as P

VMEM = pl.BlockSpec(memory_space=pltpu.VMEM)
SMEM = pl.BlockSpec(memory_space=pltpu.SMEM)
HBM = pl.BlockSpec(memory_space=pltpu.HBM)
MIB = 1024 * 1024
NT = (((1,), (1,)), ((), ()))
NN = (((1,), (0,)), ((), ()))


COST = pl.CostEstimate(flops=1, bytes_accessed=1, transcendentals=0)


def params(mib):
    return pltpu.CompilerParams(vmem_limit_bytes=mib * MIB)


def fuse(name, function, *values):
    shapes = jax.eval_shape(function, *values)

    def kernel(*refs):
        results = function(*[ref[...] for ref in refs[: len(values)]])
        for ref, result in zip(refs[len(values) :], results):
            ref[...] = result

    return pl.pallas_call(
        kernel,
        out_shape=shapes,
        in_specs=[VMEM] * len(values),
        out_specs=[VMEM] * len(shapes),
        compiler_params=params(4),
        cost_estimate=COST,
        name=name,
    )(*values)


def turn_of(slots):
    return math.gcd(slots, 8)


def product_loop(count, source_ids, target_ids, adj, source, total, dims):
    turn = turn_of(adj.shape[0])
    spare = total.shape[0] - 1
    total[...] = jnp.zeros_like(total)

    def step(index, carry):
        first = index * turn
        for k in range(turn):
            slot = first + k
            product = lax.dot_general(
                source[source_ids[slot]], adj[slot], dims, preferred_element_type=jnp.float32
            )
            target = jnp.where(slot < count, target_ids[slot], spare)
            total[target] += product
        return carry

    lax.fori_loop(0, (count + turn - 1) // turn, step, 0)


def fetch_kernel(count, rows, cols, features, tile, *refs):
    outs, (sem, small_sem) = refs[:5], refs[5:]
    half = features.shape[0] // 2
    sources = (rows, cols, features.at[pl.ds(0, half)], features.at[pl.ds(half, half)])
    small = [
        pltpu.make_async_copy(source, target, small_sem.at[n])
        for n, (source, target) in enumerate(zip(sources, outs))
    ]
    for copy in small:
        copy.start()
    turn = turn_of(tile.shape[0])

    def copy_turn(index):
        blocks = pl.ds(index * turn, turn)
        return pltpu.make_async_copy(tile.at[blocks], outs[4].at[blocks], sem.at[index])

    def begin(index, carry):
        copy_turn(index).start()
        return carry

    def wait(index, carry):
        copy_turn(index).wait()
        return carry

    turns = (count[0, 0] + turn - 1) // turn
    lax.fori_loop(0, turns, begin, 0)
    lax.fori_loop(0, turns, wait, 0)
    for copy in small:
        copy.wait()


def fetch(count, rows, cols, features, tile):
    arrays = (rows, cols, features, tile)
    half = jax.ShapeDtypeStruct((features.shape[0] // 2, features.shape[1]), features.dtype)
    outs = [jax.ShapeDtypeStruct(array.shape, array.dtype) for array in (rows, cols)] + [half] * 2
    return pl.pallas_call(
        fetch_kernel,
        out_shape=outs + [jax.ShapeDtypeStruct(tile.shape, tile.dtype)],
        in_specs=[SMEM] + [HBM] * 4,
        out_specs=[VMEM] * 5,
        scratch_shapes=[
            pltpu.SemaphoreType.DMA((tile.shape[0] // turn_of(tile.shape[0]),)),
            pltpu.SemaphoreType.DMA((4,)),
        ],
        compiler_params=params(4),
        cost_estimate=COST,
        name="fetch",
    )(count, *[pltpu.with_memory_space_constraint(array, pltpu.HBM) for array in arrays])


def forward_kernel(n_parts, depths, layout, place, count, rows, cols, adj, *refs):
    parts, refs = refs[:n_parts], refs[n_parts:]
    source, total = refs[-2:]
    outs = refs[-2 - len(depths) * len(layout) : -2]
    carried = refs[: len(refs) - 2 - len(outs)]
    size = adj.shape[1]
    row = 0
    for part in parts:
        depth = part.shape[0]
        for c in range(source.shape[0]):
            source[c, row : row + depth, :] = part[:, c * size : (c + 1) * size]
        row += depth
    product_loop(count[0, 0], cols, rows, adj, source, total, NT)
    blocks = outs[0].shape[1] // size
    ahead = carried[0].shape[0] // len(layout[0]) if carried else 0
    outs = iter(outs)
    row = 0
    for depth in depths:
        for m, chunks in enumerate(layout):
            out = next(outs)
            for n, k in enumerate(chunks):
                begin = n * (ahead + depth)
                if ahead:
                    out[begin : begin + ahead, :] = carried[m][n * ahead : (n + 1) * ahead, :]
                first = (place[0] ^ k) * blocks
                for i in range(blocks):
                    out[begin + ahead : begin + ahead + depth, i * size : (i + 1) * size] = total[
                        first + i, row : row + depth, :
                    ].astype(out.dtype)
        row += depth


def forward(place, count, rows, cols, adj, parts, row_blocks, depths, layout, carried=()):
    size = adj.shape[1]
    col_blocks = parts[0].shape[1] // size
    wide = row_blocks * size // sum(len(chunks) for chunks in layout)
    ahead = carried[0].shape[0] // len(layout[0]) if carried else 0
    outs = [
        jax.ShapeDtypeStruct((len(chunks) * (ahead + depth), wide), jnp.bfloat16)
        for depth in depths
        for chunks in layout
    ]
    return pl.pallas_call(
        functools.partial(forward_kernel, len(parts), depths, layout),
        out_shape=outs,
        in_specs=[SMEM] * 4 + [VMEM] * (1 + len(parts) + len(carried)),
        out_specs=[VMEM] * len(outs),
        scratch_shapes=[
            pltpu.VMEM((col_blocks, sum(depths), size), jnp.bfloat16),
            pltpu.VMEM((row_blocks + 1, sum(depths), size), jnp.float32),
        ],
        compiler_params=params(14),
        cost_estimate=COST,
        name="forward_products",
    )(place, count, rows, cols, adj, *parts, *carried)


def backward_kernel(spots, depths, place, count, rows, cols, adj, *refs):
    n_parts = 1 + max(part for places in spots for part, _ in places)
    parts = refs[:n_parts]
    outs = refs[n_parts:-2]
    source, total = refs[-2:]
    size = adj.shape[1]
    blocks = parts[0].shape[1] // size
    for k, places in enumerate(spots):
        first = (place[0] ^ k) * blocks
        row = 0
        for (part, offset), depth in zip(places, depths):
            for i in range(blocks):
                source[first + i, row : row + depth, :] = parts[part][
                    offset : offset + depth, i * size : (i + 1) * size
                ]
            row += depth
    product_loop(count[0, 0], rows, cols, adj, source, total, NN)
    row = 0
    for out in outs:
        depth = out.shape[0]
        for c in range(total.shape[0] - 1):
            out[:, c * size : (c + 1) * size] = total[c, row : row + depth, :].astype(out.dtype)
        row += depth


def backward(place, count, rows, cols, adj, parts, spots, depths, out_depths, col_blocks):
    size = adj.shape[1]
    row_blocks = len(spots) * parts[0].shape[1] // size
    return pl.pallas_call(
        functools.partial(backward_kernel, spots, depths),
        out_shape=[jax.ShapeDtypeStruct((depth, col_blocks * size), jnp.bfloat16) for depth in out_depths],
        in_specs=[SMEM] * 4 + [VMEM] * (1 + len(parts)),
        out_specs=[VMEM] * len(out_depths),
        scratch_shapes=[
            pltpu.VMEM((row_blocks, sum(out_depths), size), jnp.bfloat16),
            pltpu.VMEM((col_blocks + 1, sum(out_depths), size), jnp.float32),
        ],
        compiler_params=params(14),
        cost_estimate=COST,
        name="backward_products",
    )(place, count, rows, cols, adj, *parts)


def middle_kernel(sizes, order, n_sum, n_row, row, weight, cotangent, *refs):
    terms = refs[: n_sum * len(sizes)]
    outs = refs[n_sum * len(sizes) : -1]
    output, deltas, aggregated, *backs = outs
    ordered = refs[-1]
    depth = weight.shape[0] // n_row
    for j in range(n_row):
        first = pl.multiple_of((row[0] ^ j) * depth, depth)
        ordered[j * depth : (j + 1) * depth, :] = weight[pl.ds(first, depth), :]
    first = 0
    for p, size in enumerate(sizes):
        summed = terms[p * n_sum][:size, :].astype(jnp.float32)
        for k in range(1, n_sum):
            summed += terms[p * n_sum + k][:size, :].astype(jnp.float32)
        aggregated[first : first + size, :] = summed.astype(jnp.bfloat16)
        first += size
    nodes_first = aggregated[...].T
    preact = jnp.dot(nodes_first, ordered[...], preferred_element_type=jnp.float32)
    gate = jax.nn.sigmoid(preact)
    output[...] = (preact * gate).astype(jnp.bfloat16)
    slopes = gate * (1.0 + preact * (1.0 - gate))
    delta = (cotangent[...].astype(jnp.float32) * slopes).astype(jnp.bfloat16)
    deltas[...] = delta
    product = lax.dot_general(ordered[...], delta, NT, preferred_element_type=jnp.float32)
    product = jnp.concatenate([product[k * depth : (k + 1) * depth, :] for k in order]).astype(jnp.bfloat16)
    first = 0
    for back in backs:
        first %= product.shape[0]
        back[...] = product[first : first + back.shape[0], :]
        first += back.shape[0]


def middle(n_row, row, weight, cotangent, pieces, order, depths):
    sizes = [piece[0].shape[0] for piece in pieces]
    nodes = cotangent.shape[0]
    features = weight.shape[0]
    shape = jax.ShapeDtypeStruct
    outs = [
        shape((nodes, features), jnp.bfloat16),
        shape((nodes, features), jnp.bfloat16),
        shape((features, nodes), jnp.bfloat16),
    ] + [shape((depth, nodes), jnp.bfloat16) for depth in depths]
    flat = [term for piece in pieces for term in piece]
    return pl.pallas_call(
        functools.partial(middle_kernel, sizes, order, len(pieces[0]), n_row),
        out_shape=outs,
        in_specs=[SMEM] + [VMEM] * (2 + len(flat)),
        out_specs=[VMEM] * len(outs),
        scratch_shapes=[pltpu.VMEM(weight.shape, jnp.bfloat16)],
        compiler_params=params(10),
        cost_estimate=COST,
        name="layer",
    )(row, weight, cotangent, *flat)


def gradient_kernel(scale, order, aggregated, deltas, *outs):
    product = jnp.dot(aggregated[...], deltas[...], preferred_element_type=jnp.float32) * scale
    for out, chunks in zip(outs, order):
        depth = out.shape[1]
        for n, k in enumerate(chunks):
            out[n] = product[k * depth : (k + 1) * depth, :]


def gradient(scale, order, aggregated, deltas):
    depth = aggregated.shape[0] // sum(len(chunks) for chunks in order)
    outs = [jax.ShapeDtypeStruct((len(chunks), depth, deltas.shape[1]), jnp.float32) for chunks in order]
    return pl.pallas_call(
        functools.partial(gradient_kernel, scale, order),
        out_shape=outs,
        in_specs=[VMEM] * 2,
        out_specs=[VMEM] * len(outs),
        compiler_params=params(6),
        cost_estimate=COST,
        name="weight_gradient",
    )(aggregated, deltas)


def swap(value, axis, k):
    size = lax.axis_size(axis)
    return lax.ppermute(value, axis, [(i, i ^ k) for i in range(size)])


def wide_sum(*values):
    total = values[0].astype(jnp.float32)
    for value in values[1:]:
        total = total + value.astype(jnp.float32)
    return (total.astype(values[0].dtype),)


def after(value, *earlier):
    return lax.optimization_barrier((value, *earlier))[0]


def with_chunk(rows, chunk):
    high = chunk.astype(jnp.bfloat16)
    low = (chunk - high.astype(jnp.float32)).astype(jnp.bfloat16)
    return (jnp.concatenate([rows, jnp.concatenate([high, low], axis=1)]),)


def chunk_sum(depth, *values):
    total = None
    for value in values:
        halves = value[-depth:].astype(jnp.float32)
        wide = halves.shape[1] // 2
        chunk = halves[:, :wide] + halves[:, wide:]
        total = chunk if total is None else total + chunk
    return (total,)


def halves_sum(mine, *received):
    total = mine + jnp.concatenate(received)
    half = total.shape[0] // 2
    return total[:half], total[half:]


def far_sums(mine, received):
    total = mine[: received.shape[0]].astype(jnp.float32) + received.astype(jnp.float32)
    total = total.astype(mine.dtype)
    return (jnp.concatenate([total, total[:, :128]], axis=1),)


def near_kernel(row, chunk, sibling, half_way, mine, *refs):
    depth, nodes = half_way.shape[0], mine.shape[1]
    n_sums = mine.shape[0] // depth - 1
    received, (chunks, *sums) = refs[:n_sums], refs[n_sums:]
    for k, ref in enumerate((chunk, sibling)):
        wide = ref.shape[1]
        chunks[:, k * wide : (k + 1) * wide] = ref[...].astype(chunks.dtype)
    passed = half_way[:, :nodes].astype(jnp.float32)
    odd = row[0] % 2
    for n, out in enumerate(sums):
        first = (n + 1) * depth
        total = mine[first : first + depth, :].astype(jnp.float32) + received[n][...].astype(jnp.float32)
        if n:
            total += jnp.where(odd == 2 - n, passed, 0.0)
            out[:, nodes:] = chunks[...]
        out[:, :nodes] = total.astype(out.dtype)


def near_payloads(row, chunk, sibling, half_way, mine, received):
    depth, nodes = received[0].shape
    wide = 2 * chunk.shape[1]
    shapes = [(depth, wide), (depth, nodes)] + [(depth, nodes + wide)] * (len(received) - 1)
    return pl.pallas_call(
        near_kernel,
        out_shape=[jax.ShapeDtypeStruct(shape, mine.dtype) for shape in shapes],
        in_specs=[SMEM] + [VMEM] * (4 + len(received)),
        out_specs=[VMEM] * len(shapes),
        compiler_params=params(8),
        cost_estimate=COST,
        name="near_payloads",
    )(row, chunk, sibling, half_way, mine, *received)


def finish_kernel(keys, row, *refs):
    grad_features, grad_weight = refs[-2:]
    depth, nodes = grad_features.shape
    wide = grad_weight.shape[1]
    parts = [ref for ref in refs[:-2] if ref.shape[1] >= nodes]
    values = [ref[...] for ref in refs[:-2] if ref.shape[1] < nodes] + [part[:, nodes:] for part in parts[1:]]
    total = parts[0][...].astype(jnp.float32)
    for part in parts[1:]:
        total += part[:, :nodes].astype(jnp.float32)
    grad_features[...] = total.astype(grad_features.dtype)
    for key, value in zip(keys, values):
        for k in range(2):
            first = pl.multiple_of((row[0] ^ (key + k)) * depth, depth)
            grad_weight[pl.ds(first, depth), :] = value[:, k * wide : (k + 1) * wide].astype(jnp.float32)


def finish(row, keys, parts, chunks):
    depth, nodes = parts[0].shape
    return pl.pallas_call(
        functools.partial(finish_kernel, keys),
        out_shape=[
            jax.ShapeDtypeStruct((depth, nodes), jnp.bfloat16),
            jax.ShapeDtypeStruct((2 * len(keys) * depth, chunks[0].shape[1] // 2), jnp.float32),
        ],
        in_specs=[SMEM] + [VMEM] * (len(parts) + len(chunks)),
        out_specs=[VMEM] * 2,
        compiler_params=params(8),
        cost_estimate=COST,
        name="finish",
    )(row, *parts, *chunks)


def shards_exchanged(features, weight, adj_values, block_rows, block_cols, block_counts, cotangent):
    n_row = lax.axis_size("row")
    n_col = lax.axis_size("col")
    adj = adj_values[0, 0]
    rows = block_rows[0, 0]
    cols = block_cols[0, 0]
    count = block_counts
    size = adj.shape[1]
    nodes = cotangent.shape[0] * n_row * n_col
    row_blocks = cotangent.shape[0] * n_col // size
    col_blocks = features.shape[0] // size
    row = lax.axis_index("row").reshape(1)
    col = lax.axis_index("col").reshape(1)
    own = after(features.T, row, col)

    depth = features.shape[1]
    near = [k for k in range(2, n_row, 2) if k & (k - 1) == 0]
    far = [k for k in range(2, n_row, 2) if k & (k - 1) != 0]
    sibling = swap(own, "row", 1)
    from_near = [swap(own, "row", k) for k in near]
    rows, cols, *halves, tile = fetch(count, rows, cols, own, adj)
    from_near = [after(part, tile) for part in from_near]
    from_far = [swap(half, "row", k) for k in far for half in halves]

    def pass_on(beyond, received):
        return wide_sum(beyond, received[beyond.shape[0] :])

    layout = [(0,), (2,), (1, 3)]

    def fold(kept, beyond, received):
        (passed,) = fuse("pass_on", pass_on, beyond, received)
        return [kept, received, swap(passed, "col", 2)]

    n_near = 2 * depth * (1 + len(near))
    cut = n_near * 5 // 6
    parts = [own, sibling] + [piece for part in from_near for piece in (part, swap(part, "row", 1))]
    kept, beyond, sent, *carried = forward(
        col, count, rows, cols, tile, parts, row_blocks, [cut, n_near - cut], layout
    )
    received = swap(sent, "col", 1)
    from_far = [after(part, kept) for part in from_far]
    parts = []
    for n in range(0, len(from_far), 2):
        halves = from_far[n : n + 2]
        parts += halves + [swap(half, "row", 1) for half in halves]
    far_piece = forward(
        col, count, rows, cols, tile, parts, row_blocks, [2 * depth * len(far)], layout, carried
    )
    far_received = swap(far_piece[2], "col", 1)
    first = fold(kept, beyond, after(received, far_piece[0]))
    second = fold(*far_piece[:2], after(far_received, first[1]))
    sums = [first, second]

    keys = far + [0] + near
    order = keys + [k + 1 for k in keys]
    cut = weight.shape[0] // 2 + depth
    cuts = [cut, weight.shape[0] - cut]
    output, deltas, aggregated, back, *backs = middle(
        n_row, row, weight, cotangent, sums, order, [sum(cuts)] + cuts
    )
    beside = swap(back, "col", 1)
    beyond = [swap(part, "col", 2) for part in backs]

    even, *odd = gradient(1.0 / math.sqrt(nodes), [(0, 4, 2, 6), (1, 5), (3, 7)], aggregated, deltas)
    even, sent = fuse("gradient_sum", halves_sum, even, *[swap(part, "row", 1) for part in odd])
    even, sent = fuse("gradient_sum", halves_sum, even, swap(sent, "row", 2))
    beyond[0] = after(beyond[0], sent)
    even = after(even, beyond[1])
    (chunk,) = fuse("gradient_sum", lambda a, b: ((a + b)[0],), even, swap(sent, "row", 4))
    (second,) = fuse("with_chunk", with_chunk, beyond[1], chunk)
    received = [swap(beyond[0], "col", 1), swap(second, "col", 1)]

    (chunk,) = fuse("chunk_sum", functools.partial(chunk_sum, depth), second, received[1])

    parts = [back, beside, beyond[0], received[0], beyond[1], after(received[1], chunk)]
    spots = [[(part, 0), (part, cut)] for part in range(2)] + [[(part, 0), (part + 2, 0)] for part in (2, 3)]
    out_depths = [depth * len(keys)] + [depth] * len(keys)
    mine, *sent = backward(col, count, rows, cols, tile, parts, spots, cuts, out_depths, col_blocks)
    from_sibling = [swap(part, "row", 1) for part in sent]
    (chunk,) = fuse("chunk_sum", wide_sum, chunk, swap(chunk, "col", 2))

    (far_sum,) = fuse("far_sums", far_sums, mine, from_sibling[0])
    half_way = lax.ppermute(far_sum, "row", [(i, i ^ (4 if i % 2 else 2)) for i in range(n_row)])
    chunks, own_sum, *near_sums = near_payloads(
        row, chunk, swap(chunk, "row", 1), half_way, mine, from_sibling[1:]
    )
    near_sums = [swap(part, "row", k) for part, k in zip(near_sums, near)]
    far_chunks = [swap(chunks, "row", k) for k in far]
    grad_features, grad_weight = finish(row, [0] + far + near, [own_sum] + near_sums, [chunks] + far_chunks)
    return output, grad_weight, grad_features.T


def shards_gathered(features, weight, adj_values, block_rows, block_cols, block_counts, cotangent):
    n_row = lax.axis_size("row")
    n_col = lax.axis_size("col")
    adj = adj_values[0, 0]
    rows = block_rows[0, 0]
    cols = block_cols[0, 0]
    count = block_counts
    size = adj.shape[1]
    nodes = cotangent.shape[0] * n_row * n_col
    row_blocks = cotangent.shape[0] * n_col // size
    col_blocks = features.shape[0] // size
    zero = jnp.zeros((1,), jnp.int32)
    panels = lax.all_gather(features.T, "row", axis=0, tiled=True)
    (terms,) = forward(zero, count, rows, cols, adj, [panels], row_blocks, [panels.shape[0]], [(0,)])
    part = lax.psum_scatter(terms, "col", scatter_dimension=1, tiled=True)
    output, deltas, aggregated, back = middle(1, zero, weight, cotangent, [[part]], (0,), [weight.shape[0]])
    slab = lax.all_gather(back, "col", axis=1, tiled=True)
    (column_terms,) = backward(zero, count, rows, cols, adj, [slab], [[(0, 0)]], [slab.shape[0]], [slab.shape[0]], col_blocks)
    grad_features = lax.psum_scatter(column_terms, "row", scatter_dimension=0, tiled=True).T
    (part,) = gradient(1.0 / math.sqrt(nodes), [(0,)], aggregated, deltas)
    grad_weight = lax.psum(part[0], ("row", "col"))
    return output, grad_weight, grad_features


def solution(mesh):
    n_row = mesh.shape["row"]
    n_col = mesh.shape["col"]
    exchanged = n_row == 8 and n_col == 4
    return jax.shard_map(
        shards_exchanged if exchanged else shards_gathered,
        mesh=mesh,
        in_specs=(
            P("col", "row"),
            P(),
            P("row", "col", None, None, None),
            P("row", "col", None),
            P("row", "col", None),
            P("row", "col"),
            P(("row", "col"), None),
        ),
        out_specs=(P(("row", "col"), None), P(), P("col", "row")),
        check_vma=False,
    )
```

profile of v0, /device:TPU:0, one launch (start us, length us, event | category | flops | bytes accessed | tf_op | source)
XLA Modules:
  0.0 92.9 jit_solution(6548307069237955184)
XLA Ops:
  0.6 3.0 %collective-permute-start.1 = (bf16[32,4096]{1,0:T(8,128)(2,1)}, bf16[32,4096]{1,0:T(8,128)(2,1)S(1)}, u32[]{:S(2)}, u32[]{:S(2)}) collective-permute-start(bf16[32,4096]{1,0:T(8,128)(2,1)} %bitcast.7), channel_id=1, source_target_pairs={{0,8},{4,12},{8,0},{12,4},{16,24},{20,28},{24,16},{28,20},{1,9},{5... | collective-permute-start | bytes 786440 | tf_op jit(solution)/shard_map/ppermute | solution.py:297
  3.7 1.5 %collective-permute-start.3 = (bf16[32,4096]{1,0:T(8,128)(2,1)}, bf16[32,4096]{1,0:T(8,128)(2,1)S(1)}, u32[]{:S(2)}, u32[]{:S(2)}) collective-permute-start(bf16[32,4096]{1,0:T(8,128)(2,1)} %bitcast.8), channel_id=1, source_target_pairs={{0,16},{4,20},{8,24},{12,28},{16,0},{20,4},{24,8},{28,12},{1,17},{... | collective-permute-start | bytes 786440 | tf_op jit(solution)/shard_map/ppermute | solution.py:297
  5.8 1.6 %fetch.1 = (s32[96]{0:T(128)S(1)}, s32[96]{0:T(128)S(1)}, bf16[16,4096]{1,0:T(8,128)(2,1)S(1)}, bf16[16,4096]{1,0:T(8,128)(2,1)S(1)}, bf16[96,128,128]{2,1,0:T(8,128)(2,1)S(1)}) custom-call(s32[1,1]{1,0:T(1,128)S(6)} %copy.10.count, s32[96]{0:T(128)} %bitcast.13, s32[96]{0:T(128)} %bitcast.14, bf16[32,4096]{1,0:T(8,128)(2,1)} %bitcast.10, ...), custom_call_target="tpu_custom_call" | custom-call | flops 1 | bytes 1 | tf_op jit(solution)/shard_map/fetch/pallas_call | solution.py:103
  7.4 2.8 %collective-permute-done.1.refs_2_ = bf16[32,4096]{1,0:T(8,128)(2,1)S(1)} collective-permute-done((bf16[32,4096]{1,0:T(8,128)(2,1)}, bf16[32,4096]{1,0:T(8,128)(2,1)S(1)}, u32[]{:S(2)}, u32[]{:S(2)}) %collective-permute-start.1) | collective-permute-done | bytes 262176 | tf_op jit(solution)/shard_map/ppermute | solution.py:297
  10.2 1.5 %collective-permute-done.3.refs_4_ = bf16[32,4096]{1,0:T(8,128)(2,1)S(1)} collective-permute-done((bf16[32,4096]{1,0:T(8,128)(2,1)}, bf16[32,4096]{1,0:T(8,128)(2,1)S(1)}, u32[]{:S(2)}, u32[]{:S(2)}) %collective-permute-start.3) | collective-permute-done | bytes 262176 | tf_op jit(solution)/shard_map/ppermute | solution.py:297
  11.6 1.7 %collective-permute-start.7 = (bf16[16,4096]{1,0:T(8,128)(2,1)S(1)}, bf16[16,4096]{1,0:T(8,128)(2,1)S(1)}, u32[]{:S(2)}, u32[]{:S(2)}) collective-permute-start(bf16[16,4096]{1,0:T(8,128)(2,1)S(1)} %get-tuple-element.61), channel_id=1, source_target_pairs={{0,24},{4,28},{8,16},{12,20},{16,8},{20,12},{24,0},{28,4},{1,25},{... | collective-permute-start | bytes 393224 | tf_op jit(solution)/shard_map/ppermute | solution.py:297
  13.4 1.2 %collective-permute-start.6 = (bf16[16,4096]{1,0:T(8,128)(2,1)S(1)}, bf16[16,4096]{1,0:T(8,128)(2,1)S(1)}, u32[]{:S(2)}, u32[]{:S(2)}) collective-permute-start(bf16[16,4096]{1,0:T(8,128)(2,1)S(1)} %get-tuple-element.59), channel_id=1, source_target_pairs={{0,24},{4,28},{8,16},{12,20},{16,8},{20,12},{24,0},{28,4},{1,25},{... | collective-permute-start | bytes 393224 | tf_op jit(solution)/shard_map/ppermute | solution.py:297
  14.6 2.6 %forward_products.2 = (bf16[160,512]{1,0:T(8,128)(2,1)S(1)}, bf16[160,512]{1,0:T(8,128)(2,1)S(1)}, bf16[320,512]{1,0:T(8,128)(2,1)S(1)}, bf16[32,512]{1,0:T(8,12...) custom-call(s32[1]{0:T(128)} %bitcast.1.place, s32[1,1]{1,0:T(1,128)S(6)} %copy.10.count, ...), custom_call_target="tpu_custom_call" | custom-call | flops 1 | bytes 1 | tf_op jit(solution)/shard_map/forward_products/pallas_call | solution.py:160
  17.2 1.6 %collective-permute-start.5 = (bf16[320,512]{1,0:T(8,128)(2,1)S(1)}, bf16[320,512]{1,0:T(8,128)(2,1)S(1)}, u32[]{:S(2)}, u32[]{:S(2)}) collective-permute-start(bf16[320,512]{1,0:T(8,128)(2,1)S(1)} %get-tuple-element.58), channel_id=1, source_target_pairs={{0,1},{1,0},{2,3},{3,2},{4,5},{5,4},{6,7},{7,6},{8,9},{9,8},{10,11... | collective-permute-start | bytes 983048 | tf_op jit(solution)/shard_map/ppermute | solution.py:297
  18.9 1.9 %collective-permute-start.9 = (bf16[16,4096]{1,0:T(8,128)(2,1)S(1)}, bf16[16,4096]{1,0:T(8,128)(2,1)S(1)}, u32[]{:S(2)}, u32[]{:S(2)}) collective-permute-start(bf16[16,4096]{1,0:T(8,128)(2,1)S(1)} %collective-permute-done.7.refs_1_), channel_id=1, source_target_pairs={{0,4},{4,0},{8,12},{12,8},{16,20},{20,16},{24,28},{28,24},{1,5},{5... | collective-permute-start | bytes 393224 | tf_op jit(solution)/shard_map/ppermute | solution.py:297
  22.6 2.1 %forward_products.3 = (bf16[96,512]{1,0:T(8,128)(2,1)S(1)}, bf16[96,512]{1,0:T(8,128)(2,1)S(1)}, bf16[192,512]{1,0:T(8,128)(2,1)S(1)}) custom-call(s32[1]{0:T(128)} %bitcast.1.place, s32[1,1]{1,0:T(1,128)S(6)} %copy.10.count, s32[96]{0:T(128)S(1)} %get-tuple-element.52.rows, s32[96]{0:T(128)S(1)} %get-tuple-element.53.cols, ...), custom_call_target="tpu_custom_call" | custom-call | flops 1 | bytes 1 | tf_op jit(solution)/shard_map/forward_products/pallas_call | solution.py:160
  24.8 1.6 %collective-permute-start.11 = (bf16[192,512]{1,0:T(8,128)(2,1)S(1)}, bf16[192,512]{1,0:T(8,128)(2,1)S(1)}, u32[]{:S(2)}, u32[]{:S(2)}) collective-permute-start(bf16[192,512]{1,0:T(8,128)(2,1)S(1)} %get-tuple-element.69), channel_id=1, source_target_pairs={{0,1},{1,0},{2,3},{3,2},{4,5},{5,4},{6,7},{7,6},{8,9},{9,8},{10,11... | collective-permute-start | bytes 589832 | tf_op jit(solution)/shard_map/ppermute | solution.py:297
  26.9 4.8 %collective-permute-start.10 = (bf16[160,512]{1,0:T(8,128)(2,1)S(1)}, bf16[160,512]{1,0:T(8,128)(2,1)S(1)}, u32[]{:S(2)}, u32[]{:S(2)}) collective-permute-start(bf16[160,512]{1,0:T(8,128)(2,1)S(1)} %pass_on.2), channel_id=1, source_target_pairs={{0,2},{1,3},{2,0},{3,1},{4,6},{5,7},{6,4},{7,5},{8,10},{9,11},{10,... | collective-permute-start | bytes 491528 | tf_op jit(solution)/shard_map/ppermute | solution.py:297
  31.8 5.1 %collective-permute-start.12 = (bf16[96,512]{1,0:T(8,128)(2,1)S(1)}, bf16[96,512]{1,0:T(8,128)(2,1)S(1)}, u32[]{:S(2)}, u32[]{:S(2)}) collective-permute-start(bf16[96,512]{1,0:T(8,128)(2,1)S(1)} %pass_on.3), channel_id=1, source_target_pairs={{0,2},{1,3},{2,0},{3,1},{4,6},{5,7},{6,4},{7,5},{8,10},{9,11},{10,... | collective-permute-start | bytes 294920 | tf_op jit(solution)/shard_map/ppermute | solution.py:297
  36.8 6.8 %collective-permute-done.12.refs_5_ = bf16[96,512]{1,0:T(8,128)(2,1)S(1)} collective-permute-done((bf16[96,512]{1,0:T(8,128)(2,1)S(1)}, bf16[96,512]{1,0:T(8,128)(2,1)S(1)}, u32[]{:S(2)}, u32[]{:S(2)}) %collective-permute-start.12) | collective-permute-done | bytes 98336 | tf_op jit(solution)/shard_map/ppermute | solution.py:297
  43.6 1.1 %layer.1 = (bf16[512,256]{1,0:T(8,128)(2,1)}, bf16[512,256]{1,0:T(8,128)(2,1)S(1)}, bf16[256,512]{1,0:T(8,128)(2,1)S(1)}, bf16[256,512]{1,0:T(8,128)(2,1)S(1)}, ...) custom-call(s32[1]{0:T(128)} %bitcast.row, bf16[256,256]{1,0:T(8,128)(2,1)S(1)} %copy-done.2, ...), custom_call_target="tpu_custom_call" | custom-call | flops 1 | bytes 1 | tf_op jit(solution)/shard_map/layer/pallas_call | solution.py:261
  45.6 3.5 %collective-permute-start.21 = (bf16[256,512]{1,0:T(8,128)(2,1)S(1)}, bf16[256,512]{1,0:T(8,128)(2,1)S(1)}, u32[]{:S(2)}, u32[]{:S(2)}) collective-permute-start(bf16[256,512]{1,0:T(8,128)(2,1)S(1)} %get-tuple-element.84.refs_0_), channel_id=1, source_target_pairs={{0,1},{1,0},{2,3},{3,2},{4,5},{5,4},{6,7},{7,6},{8,9},{9,8},{10,11... | collective-permute-start | bytes 786440 | tf_op jit(solution)/shard_map/ppermute | solution.py:297
  49.8 3.6 %collective-permute-done.16.refs_1_ = f32[2,32,256]{2,1,0:T(8,128)S(1)} collective-permute-done((f32[2,32,256]{2,1,0:T(8,128)S(1)}, f32[2,32,256]{2,1,0:T(8,128)S(1)}, u32[]{:S(2)}, u32[]{:S(2)}) %collective-permute-start.16) | collective-permute-done | bytes 65568 | tf_op jit(solution)/shard_map/ppermute | solution.py:297
  53.6 1.5 %collective-permute-done.22.refs_2_ = bf16[160,512]{1,0:T(8,128)(2,1)S(1)} collective-permute-done((bf16[160,512]{1,0:T(8,128)(2,1)S(1)}, bf16[160,512]{1,0:T(8,128)(2,1)S(1)}, u32[]{:S(2)}, u32[]{:S(2)}) %collective-permute-start.22) | collective-permute-done | bytes 163872 | tf_op jit(solution)/shard_map/ppermute | solution.py:297
  55.1 2.7 %collective-permute-done.13.refs_0_.refs_4_ = bf16[96,512]{1,0:T(8,128)(2,1)S(1)} collective-permute-done((bf16[96,512]{1,0:T(8,128)(2,1)S(1)}, bf16[96,512]{1,0:T(8,128)(2,1)S(1)}, u32[]{:S(2)}, u32[]{:S(2)}) %collective-permute-start.13) | collective-permute-done | bytes 98336 | tf_op jit(solution)/shard_map/ppermute | solution.py:297
  57.9 2.7 %collective-permute-start.18 = (bf16[128,512]{1,0:T(8,128)(2,1)S(1)}, bf16[128,512]{1,0:T(8,128)(2,1)S(1)}, u32[]{:S(2)}, u32[]{:S(2)}) collective-permute-start(bf16[128,512]{1,0:T(8,128)(2,1)S(1)} %with_chunk.1.refs_0_), channel_id=1, source_target_pairs={{0,1},{1,0},{2,3},{3,2},{4,5},{5,4},{6,7},{7,6},{8,9},{9,8},{10,11... | collective-permute-start | bytes 393224 | tf_op jit(solution)/shard_map/ppermute | solution.py:297
  60.6 6.8 %collective-permute-done.18.refs_1_.refs_5_ = bf16[128,512]{1,0:T(8,128)(2,1)S(1)} collective-permute-done((bf16[128,512]{1,0:T(8,128)(2,1)S(1)}, bf16[128,512]{1,0:T(8,128)(2,1)S(1)}, u32[]{:S(2)}, u32[]{:S(2)}) %collective-permute-start.18) | collective-permute-done | bytes 131104 | tf_op jit(solution)/shard_map/ppermute | solution.py:297
  67.5 2.8 %backward_products.1 = (bf16[128,4096]{1,0:T(8,128)(2,1)S(1)}, bf16[32,4096]{1,0:T(8,128)(2,1)S(1)}, bf16[32,4096]{1,0:T(8,128)(2,1)S(1)}, bf16[32,4096]{1,0:T(8,128)(2,1)S(1)}, bf16[32,4096]{1,0:T(8,128)(2,1)S(1)}) custom-call(s32[1]{0:T(128)} %bitcast.1.place, s32[1,1]{1,0:T(1,128)S(6)} %copy.10.count, s32[96]{0:T(128)S(1)} %get-tuple-element.52.rows, ...), custom_call_target="tpu_custom_call" | custom-call | flops 1 | bytes 1 | tf_op jit(solution)/shard_map/backward_products/pallas_call | solution.py:203
  70.4 1.4 %collective-permute-start.24 = (bf16[32,4096]{1,0:T(8,128)(2,1)S(1)}, bf16[32,4096]{1,0:T(8,128)(2,1)S(1)}, u32[]{:S(2)}, u32[]{:S(2)}) collective-permute-start(bf16[32,4096]{1,0:T(8,128)(2,1)S(1)} %get-tuple-element.89), channel_id=1, source_target_pairs={{0,4},{4,0},{8,12},{12,8},{16,20},{20,16},{24,28},{28,24},{1,5},{5... | collective-permute-start | bytes 786440 | tf_op jit(solution)/shard_map/ppermute | solution.py:297
  71.8 1.2 %collective-permute-done.24.refs_1_ = bf16[32,4096]{1,0:T(8,128)(2,1)S(1)} collective-permute-done((bf16[32,4096]{1,0:T(8,128)(2,1)S(1)}, bf16[32,4096]{1,0:T(8,128)(2,1)S(1)}, u32[]{:S(2)}, u32[]{:S(2)}) %collective-permute-start.24) | collective-permute-done | bytes 262176 | tf_op jit(solution)/shard_map/ppermute | solution.py:297
  73.0 0.9 %collective-permute-start.25 = (bf16[32,4224]{1,0:T(8,128)(2,1)S(1)}, bf16[32,4224]{1,0:T(8,128)(2,1)S(1)}, u32[]{:S(2)}, u32[]{:S(2)}) collective-permute-start(bf16[32,4224]{1,0:T(8,128)(2,1)S(1)} %far_sums.1), channel_id=1, source_target_pairs={{0,8},{4,20},{8,0},{12,28},{16,24},{20,4},{24,16},{28,12},{1,9},{5... | collective-permute-start | bytes 811016 | tf_op jit(solution)/shard_map/ppermute | solution.py:486
  74.5 4.8 %collective-permute-done.19.refs_1_ = f32[32,256]{1,0:T(8,128)S(1)} collective-permute-done((f32[32,256]{1,0:T(8,128)S(1)}, f32[32,256]{1,0:T(8,128)S(1)}, u32[]{:S(2)}, u32[]{:S(2)}) %collective-permute-start.19) | collective-permute-done | bytes 32800 | tf_op jit(solution)/shard_map/ppermute | solution.py:297
  79.3 1.2 %collective-permute-done.20.sibling = f32[32,256]{1,0:T(8,128)S(1)} collective-permute-done((f32[32,256]{1,0:T(8,128)S(1)}, f32[32,256]{1,0:T(8,128)S(1)}, u32[]{:S(2)}, u32[]{:S(2)}) %collective-permute-start.20) | collective-permute-done | bytes 32800 | tf_op jit(solution)/shard_map/ppermute | solution.py:297
  81.1 1.5 %collective-permute-start.29 = (bf16[32,4608]{1,0:T(8,128)(2,1)S(1)}, bf16[32,4608]{1,0:T(8,128)(2,1)S(1)}, u32[]{:S(2)}, u32[]{:S(2)}) collective-permute-start(bf16[32,4608]{1,0:T(8,128)(2,1)S(1)} %get-tuple-element.94), channel_id=1, source_target_pairs={{0,8},{4,12},{8,0},{12,4},{16,24},{20,28},{24,16},{28,20},{1,9},{5... | collective-permute-start | bytes 884744 | tf_op jit(solution)/shard_map/ppermute | solution.py:297
  83.1 1.5 %collective-permute-start.31 = (bf16[32,512]{1,0:T(8,128)(2,1)S(1)}, bf16[32,512]{1,0:T(8,128)(2,1)S(1)}, u32[]{:S(2)}, u32[]{:S(2)}) collective-permute-start(bf16[32,512]{1,0:T(8,128)(2,1)S(1)} %get-tuple-element.96.refs_3_), channel_id=1, source_target_pairs={{0,24},{4,28},{8,16},{12,20},{16,8},{20,12},{24,0},{28,4},{1,25},{... | collective-permute-start | bytes 98312 | tf_op jit(solution)/shard_map/ppermute | solution.py:297
  84.6 7.1 %collective-permute-done.31.refs_4_ = bf16[32,512]{1,0:T(8,128)(2,1)S(1)} collective-permute-done((bf16[32,512]{1,0:T(8,128)(2,1)S(1)}, bf16[32,512]{1,0:T(8,128)(2,1)S(1)}, u32[]{:S(2)}, u32[]{:S(2)}) %collective-permute-start.31) | collective-permute-done | bytes 32800 | tf_op jit(solution)/shard_map/ppermute | solution.py:297
  92.0 0.9 finish.1
  (55 shorter events, 6.2 us)
Async XLA Ops:
  0.6 9.5 %collective-permute-start.1 = (bf16[32,4096]{1,0:T(8,128)(2,1)}, bf16[32,4096]{1,0:T(8,128)(2,1)S(1)}, u32[]{:S(2)}, u32[]{:S(2)}) collective-permute-start(bf16[32,4096]{1,0:T(8,128)(2,1)} %bitcast.7), channel_id=1, source_target_pairs={{0,8},{4,12},{8,0},{12,4},{16,24},{20,28},{24,16},{28,20},{1,9},{5... | collective-permute-start | bytes 786440 | tf_op jit(solution)/shard_map/ppermute | solution.py:297
  3.7 8.0 %collective-permute-start.3 = (bf16[32,4096]{1,0:T(8,128)(2,1)}, bf16[32,4096]{1,0:T(8,128)(2,1)S(1)}, u32[]{:S(2)}, u32[]{:S(2)}) collective-permute-start(bf16[32,4096]{1,0:T(8,128)(2,1)} %bitcast.8), channel_id=1, source_target_pairs={{0,16},{4,20},{8,24},{12,28},{16,0},{20,4},{24,8},{28,12},{1,17},{... | collective-permute-start | bytes 786440 | tf_op jit(solution)/shard_map/ppermute | solution.py:297
  5.2 9.4 %collective-permute-start = (bf16[32,4096]{1,0:T(8,128)(2,1)}, bf16[32,4096]{1,0:T(8,128)(2,1)S(1)}, u32[]{:S(2)}, u32[]{:S(2)}) collective-permute-start(bf16[32,4096]{1,0:T(8,128)(2,1)} %bitcast.9), channel_id=1, source_target_pairs={{0,4},{4,0},{8,12},{12,8},{16,20},{20,16},{24,28},{28,24},{1,5},{5... | collective-permute-start | bytes 786440 | tf_op jit(solution)/shard_map/ppermute | solution.py:297
  10.2 4.4 %collective-permute-start.2 = (bf16[32,4096]{1,0:T(8,128)(2,1)S(1)}, bf16[32,4096]{1,0:T(8,128)(2,1)S(1)}, u32[]{:S(2)}, u32[]{:S(2)}) collective-permute-start(bf16[32,4096]{1,0:T(8,128)(2,1)S(1)} %collective-permute-done.1.refs_2_), channel_id=1, source_target_pairs={{0,4},{4,0},{8,12},{12,8},{16,20},{20,16},{24,28},{28,24},{1,5},{5... | collective-permute-start | bytes 786440 | tf_op jit(solution)/shard_map/ppermute | solution.py:297
  11.6 2.9 %collective-permute-start.4 = (bf16[32,4096]{1,0:T(8,128)(2,1)S(1)}, bf16[32,4096]{1,0:T(8,128)(2,1)S(1)}, u32[]{:S(2)}, u32[]{:S(2)}) collective-permute-start(bf16[32,4096]{1,0:T(8,128)(2,1)S(1)} %collective-permute-done.3.refs_4_), channel_id=1, source_target_pairs={{0,4},{4,0},{8,12},{12,8},{16,20},{20,16},{24,28},{28,24},{1,5},{5... | collective-permute-start | bytes 786440 | tf_op jit(solution)/shard_map/ppermute | solution.py:297
  11.6 7.2 %collective-permute-start.7 = (bf16[16,4096]{1,0:T(8,128)(2,1)S(1)}, bf16[16,4096]{1,0:T(8,128)(2,1)S(1)}, u32[]{:S(2)}, u32[]{:S(2)}) collective-permute-start(bf16[16,4096]{1,0:T(8,128)(2,1)S(1)} %get-tuple-element.61), channel_id=1, source_target_pairs={{0,24},{4,28},{8,16},{12,20},{16,8},{20,12},{24,0},{28,4},{1,25},{... | collective-permute-start | bytes 393224 | tf_op jit(solution)/shard_map/ppermute | solution.py:297
  13.4 7.9 %collective-permute-start.6 = (bf16[16,4096]{1,0:T(8,128)(2,1)S(1)}, bf16[16,4096]{1,0:T(8,128)(2,1)S(1)}, u32[]{:S(2)}, u32[]{:S(2)}) collective-permute-start(bf16[16,4096]{1,0:T(8,128)(2,1)S(1)} %get-tuple-element.59), channel_id=1, source_target_pairs={{0,24},{4,28},{8,16},{12,20},{16,8},{20,12},{24,0},{28,4},{1,25},{... | collective-permute-start | bytes 393224 | tf_op jit(solution)/shard_map/ppermute | solution.py:297
  17.2 9.6 %collective-permute-start.5 = (bf16[320,512]{1,0:T(8,128)(2,1)S(1)}, bf16[320,512]{1,0:T(8,128)(2,1)S(1)}, u32[]{:S(2)}, u32[]{:S(2)}) collective-permute-start(bf16[320,512]{1,0:T(8,128)(2,1)S(1)} %get-tuple-element.58), channel_id=1, source_target_pairs={{0,1},{1,0},{2,3},{3,2},{4,5},{5,4},{6,7},{7,6},{8,9},{9,8},{10,11... | collective-permute-start | bytes 983048 | tf_op jit(solution)/shard_map/ppermute | solution.py:297
  18.9 2.9 %collective-permute-start.9 = (bf16[16,4096]{1,0:T(8,128)(2,1)S(1)}, bf16[16,4096]{1,0:T(8,128)(2,1)S(1)}, u32[]{:S(2)}, u32[]{:S(2)}) collective-permute-start(bf16[16,4096]{1,0:T(8,128)(2,1)S(1)} %collective-permute-done.7.refs_1_), channel_id=1, source_target_pairs={{0,4},{4,0},{8,12},{12,8},{16,20},{20,16},{24,28},{28,24},{1,5},{5... | collective-permute-start | bytes 393224 | tf_op jit(solution)/shard_map/ppermute | solution.py:297
  21.2 1.3 %collective-permute-start.8 = (bf16[16,4096]{1,0:T(8,128)(2,1)S(1)}, bf16[16,4096]{1,0:T(8,128)(2,1)S(1)}, u32[]{:S(2)}, u32[]{:S(2)}) collective-permute-start(bf16[16,4096]{1,0:T(8,128)(2,1)S(1)} %collective-permute-done.6.refs_0_), channel_id=1, source_target_pairs={{0,4},{4,0},{8,12},{12,8},{16,20},{20,16},{24,28},{28,24},{1,5},{5... | collective-permute-start | bytes 393224 | tf_op jit(solution)/shard_map/ppermute | solution.py:297
  24.8 7.0 %collective-permute-start.11 = (bf16[192,512]{1,0:T(8,128)(2,1)S(1)}, bf16[192,512]{1,0:T(8,128)(2,1)S(1)}, u32[]{:S(2)}, u32[]{:S(2)}) collective-permute-start(bf16[192,512]{1,0:T(8,128)(2,1)S(1)} %get-tuple-element.69), channel_id=1, source_target_pairs={{0,1},{1,0},{2,3},{3,2},{4,5},{5,4},{6,7},{7,6},{8,9},{9,8},{10,11... | collective-permute-start | bytes 589832 | tf_op jit(solution)/shard_map/ppermute | solution.py:297
  26.9 16.7 %collective-permute-start.10 = (bf16[160,512]{1,0:T(8,128)(2,1)S(1)}, bf16[160,512]{1,0:T(8,128)(2,1)S(1)}, u32[]{:S(2)}, u32[]{:S(2)}) collective-permute-start(bf16[160,512]{1,0:T(8,128)(2,1)S(1)} %pass_on.2), channel_id=1, source_target_pairs={{0,2},{1,3},{2,0},{3,1},{4,6},{5,7},{6,4},{7,5},{8,10},{9,11},{10,... | collective-permute-start | bytes 491528 | tf_op jit(solution)/shard_map/ppermute | solution.py:297
  31.8 11.8 %collective-permute-start.12 = (bf16[96,512]{1,0:T(8,128)(2,1)S(1)}, bf16[96,512]{1,0:T(8,128)(2,1)S(1)}, u32[]{:S(2)}, u32[]{:S(2)}) collective-permute-start(bf16[96,512]{1,0:T(8,128)(2,1)S(1)} %pass_on.3), channel_id=1, source_target_pairs={{0,2},{1,3},{2,0},{3,1},{4,6},{5,7},{6,4},{7,5},{8,10},{9,11},{10,... | collective-permute-start | bytes 294920 | tf_op jit(solution)/shard_map/ppermute | solution.py:297
  44.7 10.3 %collective-permute-start.22 = (bf16[160,512]{1,0:T(8,128)(2,1)S(1)}, bf16[160,512]{1,0:T(8,128)(2,1)S(1)}, u32[]{:S(2)}, u32[]{:S(2)}) collective-permute-start(bf16[160,512]{1,0:T(8,128)(2,1)S(1)} %get-tuple-element.85), channel_id=1, source_target_pairs={{0,2},{1,3},{2,0},{3,1},{4,6},{5,7},{6,4},{7,5},{8,10},{9,11},{10,... | collective-permute-start | bytes 491528 | tf_op jit(solution)/shard_map/ppermute | solution.py:297
  45.0 4.1 %collective-permute-start.14 = (f32[2,32,256]{2,1,0:T(8,128)S(1)}, f32[2,32,256]{2,1,0:T(8,128)S(1)}, u32[]{:S(2)}, u32[]{:S(2)}) collective-permute-start(f32[2,32,256]{2,1,0:T(8,128)S(1)} %get-tuple-element.77), channel_id=1, source_target_pairs={{0,4},{4,0},{8,12},{12,8},{16,20},{20,16},{24,28},{28,24},{1,5},{5... | collective-permute-start | bytes 196616 | tf_op jit(solution)/shard_map/ppermute | solution.py:297
  45.2 3.9 %collective-permute-start.15 = (f32[2,32,256]{2,1,0:T(8,128)S(1)}, f32[2,32,256]{2,1,0:T(8,128)S(1)}, u32[]{:S(2)}, u32[]{:S(2)}) collective-permute-start(f32[2,32,256]{2,1,0:T(8,128)S(1)} %get-tuple-element.78), channel_id=1, source_target_pairs={{0,4},{4,0},{8,12},{12,8},{16,20},{20,16},{24,28},{28,24},{1,5},{5... | collective-permute-start | bytes 196616 | tf_op jit(solution)/shard_map/ppermute | solution.py:297
  45.6 21.9 %collective-permute-start.21 = (bf16[256,512]{1,0:T(8,128)(2,1)S(1)}, bf16[256,512]{1,0:T(8,128)(2,1)S(1)}, u32[]{:S(2)}, u32[]{:S(2)}) collective-permute-start(bf16[256,512]{1,0:T(8,128)(2,1)S(1)} %get-tuple-element.84.refs_0_), channel_id=1, source_target_pairs={{0,1},{1,0},{2,3},{3,2},{4,5},{5,4},{6,7},{7,6},{8,9},{9,8},{10,11... | collective-permute-start | bytes 786440 | tf_op jit(solution)/shard_map/ppermute | solution.py:297
  49.1 8.8 %collective-permute-start.13 = (bf16[96,512]{1,0:T(8,128)(2,1)S(1)}, bf16[96,512]{1,0:T(8,128)(2,1)S(1)}, u32[]{:S(2)}, u32[]{:S(2)}) collective-permute-start(bf16[96,512]{1,0:T(8,128)(2,1)S(1)} %get-tuple-element.73), channel_id=1, source_target_pairs={{0,2},{1,3},{2,0},{3,1},{4,6},{5,7},{6,4},{7,5},{8,10},{9,11},{10,... | collective-permute-start | bytes 294920 | tf_op jit(solution)/shard_map/ppermute | solution.py:297
  49.1 4.3 %collective-permute-start.16 = (f32[2,32,256]{2,1,0:T(8,128)S(1)}, f32[2,32,256]{2,1,0:T(8,128)S(1)}, u32[]{:S(2)}, u32[]{:S(2)}) collective-permute-start(f32[2,32,256]{2,1,0:T(8,128)S(1)} %get-tuple-element.80), channel_id=1, source_target_pairs={{0,8},{4,12},{8,0},{12,4},{16,24},{20,28},{24,16},{28,20},{1,9},{5... | collective-permute-start | bytes 196616 | tf_op jit(solution)/shard_map/ppermute | solution.py:297
  53.5 4.4 %collective-permute-start.17 = (f32[1,32,256]{2,1,0:T(8,128)S(1)}, f32[1,32,256]{2,1,0:T(8,128)S(1)}, u32[]{:S(2)}, u32[]{:S(2)}) collective-permute-start(f32[1,32,256]{2,1,0:T(8,128)S(1)} %get-tuple-element.83), channel_id=1, source_target_pairs={{0,16},{4,20},{8,24},{12,28},{16,0},{20,4},{24,8},{28,12},{1,17},{... | collective-permute-start | bytes 98312 | tf_op jit(solution)/shard_map/ppermute | solution.py:297
  55.1 12.4 %collective-permute-start.23 = (bf16[160,512]{1,0:T(8,128)(2,1)S(1)}, bf16[160,512]{1,0:T(8,128)(2,1)S(1)}, u32[]{:S(2)}, u32[]{:S(2)}) collective-permute-start(bf16[160,512]{1,0:T(8,128)(2,1)S(1)} %collective-permute-done.22.refs_2_), channel_id=1, source_target_pairs={{0,1},{1,0},{2,3},{3,2},{4,5},{5,4},{6,7},{7,6},{8,9},{9,8},{10,11... | collective-permute-start | bytes 491528 | tf_op jit(solution)/shard_map/ppermute | solution.py:297
  57.9 9.6 %collective-permute-start.18 = (bf16[128,512]{1,0:T(8,128)(2,1)S(1)}, bf16[128,512]{1,0:T(8,128)(2,1)S(1)}, u32[]{:S(2)}, u32[]{:S(2)}) collective-permute-start(bf16[128,512]{1,0:T(8,128)(2,1)S(1)} %with_chunk.1.refs_0_), channel_id=1, source_target_pairs={{0,1},{1,0},{2,3},{3,2},{4,5},{5,4},{6,7},{7,6},{8,9},{9,8},{10,11... | collective-permute-start | bytes 393224 | tf_op jit(solution)/shard_map/ppermute | solution.py:297
  70.4 2.6 %collective-permute-start.24 = (bf16[32,4096]{1,0:T(8,128)(2,1)S(1)}, bf16[32,4096]{1,0:T(8,128)(2,1)S(1)}, u32[]{:S(2)}, u32[]{:S(2)}) collective-permute-start(bf16[32,4096]{1,0:T(8,128)(2,1)S(1)} %get-tuple-element.89), channel_id=1, source_target_pairs={{0,4},{4,0},{8,12},{12,8},{16,20},{20,16},{24,28},{28,24},{1,5},{5... | collective-permute-start | bytes 786440 | tf_op jit(solution)/shard_map/ppermute | solution.py:297
  73.0 7.5 %collective-permute-start.25 = (bf16[32,4224]{1,0:T(8,128)(2,1)S(1)}, bf16[32,4224]{1,0:T(8,128)(2,1)S(1)}, u32[]{:S(2)}, u32[]{:S(2)}) collective-permute-start(bf16[32,4224]{1,0:T(8,128)(2,1)S(1)} %far_sums.1), channel_id=1, source_target_pairs={{0,8},{4,20},{8,0},{12,28},{16,24},{20,4},{24,16},{28,12},{1,9},{5... | collective-permute-start | bytes 811016 | tf_op jit(solution)/shard_map/ppermute | solution.py:486
  73.9 6.5 %collective-permute-start.26 = (bf16[32,4096]{1,0:T(8,128)(2,1)S(1)}, bf16[32,4096]{1,0:T(8,128)(2,1)S(1)}, u32[]{:S(2)}, u32[]{:S(2)}) collective-permute-start(bf16[32,4096]{1,0:T(8,128)(2,1)S(1)} %get-tuple-element.90), channel_id=1, source_target_pairs={{0,4},{4,0},{8,12},{12,8},{16,20},{20,16},{24,28},{28,24},{1,5},{5... | collective-permute-start | bytes 786440 | tf_op jit(solution)/shard_map/ppermute | solution.py:297
  73.9 6.5 %collective-permute-start.27 = (bf16[32,4096]{1,0:T(8,128)(2,1)S(1)}, bf16[32,4096]{1,0:T(8,128)(2,1)S(1)}, u32[]{:S(2)}, u32[]{:S(2)}) collective-permute-start(bf16[32,4096]{1,0:T(8,128)(2,1)S(1)} %get-tuple-element.91), channel_id=1, source_target_pairs={{0,4},{4,0},{8,12},{12,8},{16,20},{20,16},{24,28},{28,24},{1,5},{5... | collective-permute-start | bytes 786440 | tf_op jit(solution)/shard_map/ppermute | solution.py:297
  74.4 6.0 %collective-permute-start.28 = (bf16[32,4096]{1,0:T(8,128)(2,1)S(1)}, bf16[32,4096]{1,0:T(8,128)(2,1)S(1)}, u32[]{:S(2)}, u32[]{:S(2)}) collective-permute-start(bf16[32,4096]{1,0:T(8,128)(2,1)S(1)} %get-tuple-element.92), channel_id=1, source_target_pairs={{0,4},{4,0},{8,12},{12,8},{16,20},{20,16},{24,28},{28,24},{1,5},{5... | collective-permute-start | bytes 786440 | tf_op jit(solution)/shard_map/ppermute | solution.py:297
  74.4 4.8 %collective-permute-start.19 = (f32[32,256]{1,0:T(8,128)S(1)}, f32[32,256]{1,0:T(8,128)S(1)}, u32[]{:S(2)}, u32[]{:S(2)}) collective-permute-start(f32[32,256]{1,0:T(8,128)S(1)} %chunk_sum.2.refs_0_), channel_id=1, source_target_pairs={{0,2},{1,3},{2,0},{3,1},{4,6},{5,7},{6,4},{7,5},{8,10},{9,11},{10,... | collective-permute-start | bytes 98312 | tf_op jit(solution)/shard_map/ppermute | solution.py:297
  79.3 1.2 %collective-permute-start.20 = (f32[32,256]{1,0:T(8,128)S(1)}, f32[32,256]{1,0:T(8,128)S(1)}, u32[]{:S(2)}, u32[]{:S(2)}) collective-permute-start(f32[32,256]{1,0:T(8,128)S(1)} %chunk_sum.3.chunk), channel_id=1, source_target_pairs={{0,4},{4,0},{8,12},{12,8},{16,20},{20,16},{24,28},{28,24},{1,5},{5... | collective-permute-start | bytes 98312 | tf_op jit(solution)/shard_map/ppermute | solution.py:297
  81.1 10.6 %collective-permute-start.29 = (bf16[32,4608]{1,0:T(8,128)(2,1)S(1)}, bf16[32,4608]{1,0:T(8,128)(2,1)S(1)}, u32[]{:S(2)}, u32[]{:S(2)}) collective-permute-start(bf16[32,4608]{1,0:T(8,128)(2,1)S(1)} %get-tuple-element.94), channel_id=1, source_target_pairs={{0,8},{4,12},{8,0},{12,4},{16,24},{20,28},{24,16},{28,20},{1,9},{5... | collective-permute-start | bytes 884744 | tf_op jit(solution)/shard_map/ppermute | solution.py:297
  82.6 9.5 %collective-permute-start.30 = (bf16[32,4608]{1,0:T(8,128)(2,1)S(1)}, bf16[32,4608]{1,0:T(8,128)(2,1)S(1)}, u32[]{:S(2)}, u32[]{:S(2)}) collective-permute-start(bf16[32,4608]{1,0:T(8,128)(2,1)S(1)} %get-tuple-element.95), channel_id=1, source_target_pairs={{0,16},{4,20},{8,24},{12,28},{16,0},{20,4},{24,8},{28,12},{1,17},{... | collective-permute-start | bytes 884744 | tf_op jit(solution)/shard_map/ppermute | solution.py:297
  83.1 8.6 %collective-permute-start.31 = (bf16[32,512]{1,0:T(8,128)(2,1)S(1)}, bf16[32,512]{1,0:T(8,128)(2,1)S(1)}, u32[]{:S(2)}, u32[]{:S(2)}) collective-permute-start(bf16[32,512]{1,0:T(8,128)(2,1)S(1)} %get-tuple-element.96.refs_3_), channel_id=1, source_target_pairs={{0,24},{4,28},{8,16},{12,20},{16,8},{20,12},{24,0},{28,4},{1,25},{... | collective-permute-start | bytes 98312 | tf_op jit(solution)/shard_map/ppermute | solution.py:297
  (3 other events, 66.8 us)
where the time goes:
time: 92.2 us; the launch traced here: 92.9 us
  waiting for transfers between devices  42.7 us (46%)
  starting transfers between devices  36.6 us (40%)
  Pallas kernels  12.2 us (13%)
  between operations  1.48 us (2%)
    ppermute x31, waiting for transfers between devices, swap(): return lax.ppermute(value, axis, [(i, i ^ k) for i in range(size)])  42.7 us
    ppermute x31, starting transfers between devices, swap(): return lax.ppermute(value, axis, [(i, i ^ k) for i in range(size)])  35.7 us
    pallas_call x2, Pallas kernels, forward(): pl.pallas_call(functools.partial(forward_kernel, len(parts), depths, layo...  4.76 us
    pallas_call x1, Pallas kernels, backward(): pl.pallas_call(functools.partial(backward_kernel, spots, depths), out_sha...  2.84 us
  transfers between devices with their start and end apart: 32, of which 16 were waited for; matrix products, arithmetic and copies ran while one was open for 0% of the time, Pallas kernels for 7%

commit v1 on v0

--- a/solution.py
+++ b/solution.py
@@ -468,10 +468,11 @@
     even, sent = fuse("gradient_sum", halves_sum, even, *[swap(part, "row", 1) for part in odd])
     even, sent = fuse("gradient_sum", halves_sum, even, swap(sent, "row", 2))
     beyond[0] = after(beyond[0], sent)
-    even = after(even, beyond[1])
+    received = [swap(beyond[0], "col", 1)]
+    even = after(even, beyond[1], beside)
     (chunk,) = fuse("gradient_sum", lambda a, b: ((a + b)[0],), even, swap(sent, "row", 4))
     (second,) = fuse("with_chunk", with_chunk, beyond[1], chunk)
-    received = [swap(beyond[0], "col", 1), swap(second, "col", 1)]
+    received.append(swap(second, "col", 1))
 
     (chunk,) = fuse("chunk_sum", functools.partial(chunk_sum, depth), second, received[1])
 
@@ -482,6 +483,7 @@
     from_sibling = [swap(part, "row", 1) for part in sent]
     (chunk,) = fuse("chunk_sum", wide_sum, chunk, swap(chunk, "col", 2))
 
+    mine = after(mine, chunk)
     (far_sum,) = fuse("far_sums", far_sums, mine, from_sibling[0])
     half_way = lax.ppermute(far_sum, "row", [(i, i ^ (4 if i % 2 else 2)) for i in range(n_row)])
     chunks, own_sum, *near_sums = near_payloads(

time: 92.2 us -> 92.4 us (level)
  Pallas kernels: 12.2 us -> 11.2 us
    ppermute x31, starting transfers between devices: 35.7 us -> 34.5 us  [swap(): return lax.ppermute(value, axis, [(i, i ^ k) for i in range(size)])]
    ppermute x1, starting transfers between devices: 0.93 us -> 2.08 us  [shards_exchanged(): lax.ppermute(far_sum, 'row', [(i, i ^ (4 if i % 2 else 2)) for i in range...]
  transfers between devices with their start and end apart: 32 -> 32, of which waited for: 16 -> 17; matrix products, arithmetic and copies ran while one was open for 0% -> 0% of each run, Pallas kernels for 7% -> 6%
where the time goes in v1:
time: 92.4 us; the launch traced here: 92.9 us
  waiting for transfers between devices  43.6 us (47%)
  starting transfers between devices  36.6 us (40%)
  Pallas kernels  11.2 us (12%)
  between operations  1.47 us (2%)
    ppermute x31, waiting for transfers between devices, swap(): return lax.ppermute(value, axis, [(i, i ^ k) for i in range(size)])  43.4 us
    ppermute x31, starting transfers between devices, swap(): return lax.ppermute(value, axis, [(i, i ^ k) for i in range(size)])  34.5 us
    pallas_call x2, Pallas kernels, forward(): pl.pallas_call(functools.partial(forward_kernel, len(parts), depths, layo...  4.16 us
    pallas_call x1, Pallas kernels, backward(): pl.pallas_call(functools.partial(backward_kernel, spots, depths), out_sha...  2.54 us
    ppermute x1, starting transfers between devices, shards_exchanged(): lax.ppermute(far_sum, 'row', [(i, i ^ (4 if i % 2 else 2)) for i in range...  2.08 us
  transfers between devices with their start and end apart: 32, of which 17 were waited for; matrix products, arithmetic and copies ran while one was open for 0% of the time, Pallas kernels for 6%

profile of v1, /device:TPU:0, one launch (start us, length us, event | category | flops | bytes accessed | tf_op | source)
XLA Modules:
  0.0 92.9 jit_solution(14508526376638833573)
XLA Ops:
  0.6 3.0 %collective-permute-start.3 = (bf16[32,4096]{1,0:T(8,128)(2,1)}, bf16[32,4096]{1,0:T(8,128)(2,1)S(1)}, u32[]{:S(2)}, u32[]{:S(2)}) collective-permute-start(bf16[32,4096]{1,0:T(8,128)(2,1)} %bitcast.7), channel_id=1, source_target_pairs={{0,16},{4,20},{8,24},{12,28},{16,0},{20,4},{24,8},{28,12},{1,17},{... | collective-permute-start | bytes 786440 | tf_op jit(solution)/shard_map/ppermute | solution.py:297
  3.7 1.5 %collective-permute-start.1 = (bf16[32,4096]{1,0:T(8,128)(2,1)}, bf16[32,4096]{1,0:T(8,128)(2,1)S(1)}, u32[]{:S(2)}, u32[]{:S(2)}) collective-permute-start(bf16[32,4096]{1,0:T(8,128)(2,1)} %bitcast.8), channel_id=1, source_target_pairs={{0,8},{4,12},{8,0},{12,4},{16,24},{20,28},{24,16},{28,20},{1,9},{5... | collective-permute-start | bytes 786440 | tf_op jit(solution)/shard_map/ppermute | solution.py:297
  5.8 1.5 %fetch.1 = (s32[96]{0:T(128)S(1)}, s32[96]{0:T(128)S(1)}, bf16[16,4096]{1,0:T(8,128)(2,1)S(1)}, bf16[16,4096]{1,0:T(8,128)(2,1)S(1)}, bf16[96,128,128]{2,1,0:T(8,128)(2,1)S(1)}) custom-call(s32[1,1]{1,0:T(1,128)S(6)} %copy.10.count, s32[96]{0:T(128)} %bitcast.13, s32[96]{0:T(128)} %bitcast.14, bf16[32,4096]{1,0:T(8,128)(2,1)} %bitcast.10, ...), custom_call_target="tpu_custom_call" | custom-call | flops 1 | bytes 1 | tf_op jit(solution)/shard_map/fetch/pallas_call | solution.py:103
  7.3 2.9 %collective-permute-done.3.refs_4_ = bf16[32,4096]{1,0:T(8,128)(2,1)S(1)} collective-permute-done((bf16[32,4096]{1,0:T(8,128)(2,1)}, bf16[32,4096]{1,0:T(8,128)(2,1)S(1)}, u32[]{:S(2)}, u32[]{:S(2)}) %collective-permute-start.3) | collective-permute-done | bytes 262176 | tf_op jit(solution)/shard_map/ppermute | solution.py:297
  10.2 1.5 %collective-permute-done.1.refs_2_ = bf16[32,4096]{1,0:T(8,128)(2,1)S(1)} collective-permute-done((bf16[32,4096]{1,0:T(8,128)(2,1)}, bf16[32,4096]{1,0:T(8,128)(2,1)S(1)}, u32[]{:S(2)}, u32[]{:S(2)}) %collective-permute-start.1) | collective-permute-done | bytes 262176 | tf_op jit(solution)/shard_map/ppermute | solution.py:297
  12.2 1.4 %collective-permute-start.7 = (bf16[16,4096]{1,0:T(8,128)(2,1)S(1)}, bf16[16,4096]{1,0:T(8,128)(2,1)S(1)}, u32[]{:S(2)}, u32[]{:S(2)}) collective-permute-start(bf16[16,4096]{1,0:T(8,128)(2,1)S(1)} %get-tuple-element.62), channel_id=1, source_target_pairs={{0,24},{4,28},{8,16},{12,20},{16,8},{20,12},{24,0},{28,4},{1,25},{... | collective-permute-start | bytes 393224 | tf_op jit(solution)/shard_map/ppermute | solution.py:297
  13.6 1.5 %collective-permute-start.6 = (bf16[16,4096]{1,0:T(8,128)(2,1)S(1)}, bf16[16,4096]{1,0:T(8,128)(2,1)S(1)}, u32[]{:S(2)}, u32[]{:S(2)}) collective-permute-start(bf16[16,4096]{1,0:T(8,128)(2,1)S(1)} %get-tuple-element.60), channel_id=1, source_target_pairs={{0,24},{4,28},{8,16},{12,20},{16,8},{20,12},{24,0},{28,4},{1,25},{... | collective-permute-start | bytes 393224 | tf_op jit(solution)/shard_map/ppermute | solution.py:297
  15.1 2.3 %forward_products.2 = (bf16[160,512]{1,0:T(8,128)(2,1)S(1)}, bf16[160,512]{1,0:T(8,128)(2,1)S(1)}, bf16[320,512]{1,0:T(8,128)(2,1)S(1)}, bf16[32,512]{1,0:T(8,12...) custom-call(s32[1]{0:T(128)} %bitcast.1.place, s32[1,1]{1,0:T(1,128)S(6)} %copy.10.count, ...), custom_call_target="tpu_custom_call" | custom-call | flops 1 | bytes 1 | tf_op jit(solution)/shard_map/forward_products/pallas_call | solution.py:160
  17.4 1.3 %collective-permute-start.5 = (bf16[320,512]{1,0:T(8,128)(2,1)S(1)}, bf16[320,512]{1,0:T(8,128)(2,1)S(1)}, u32[]{:S(2)}, u32[]{:S(2)}) collective-permute-start(bf16[320,512]{1,0:T(8,128)(2,1)S(1)} %get-tuple-element.59), channel_id=1, source_target_pairs={{0,1},{1,0},{2,3},{3,2},{4,5},{5,4},{6,7},{7,6},{8,9},{9,8},{10,11... | collective-permute-start | bytes 983048 | tf_op jit(solution)/shard_map/ppermute | solution.py:297
  19.4 1.8 %collective-permute-done.6.refs_0_ = bf16[16,4096]{1,0:T(8,128)(2,1)S(1)} collective-permute-done((bf16[16,4096]{1,0:T(8,128)(2,1)S(1)}, bf16[16,4096]{1,0:T(8,128)(2,1)S(1)}, u32[]{:S(2)}, u32[]{:S(2)}) %collective-permute-start.6) | collective-permute-done | bytes 131104 | tf_op jit(solution)/shard_map/ppermute | solution.py:297
  22.8 1.9 %forward_products.3 = (bf16[96,512]{1,0:T(8,128)(2,1)S(1)}, bf16[96,512]{1,0:T(8,128)(2,1)S(1)}, bf16[192,512]{1,0:T(8,128)(2,1)S(1)}) custom-call(s32[1]{0:T(128)} %bitcast.1.place, s32[1,1]{1,0:T(1,128)S(6)} %copy.10.count, s32[96]{0:T(128)S(1)} %get-tuple-element.53.rows, s32[96]{0:T(128)S(1)} %get-tuple-element.54.cols, ...), custom_call_target="tpu_custom_call" | custom-call | flops 1 | bytes 1 | tf_op jit(solution)/shard_map/forward_products/pallas_call | solution.py:160
  24.7 1.4 %collective-permute-start.11 = (bf16[192,512]{1,0:T(8,128)(2,1)S(1)}, bf16[192,512]{1,0:T(8,128)(2,1)S(1)}, u32[]{:S(2)}, u32[]{:S(2)}) collective-permute-start(bf16[192,512]{1,0:T(8,128)(2,1)S(1)} %get-tuple-element.70), channel_id=1, source_target_pairs={{0,1},{1,0},{2,3},{3,2},{4,5},{5,4},{6,7},{7,6},{8,9},{9,8},{10,11... | collective-permute-start | bytes 589832 | tf_op jit(solution)/shard_map/ppermute | solution.py:297
  26.6 2.7 %collective-permute-start.10 = (bf16[160,512]{1,0:T(8,128)(2,1)S(1)}, bf16[160,512]{1,0:T(8,128)(2,1)S(1)}, u32[]{:S(2)}, u32[]{:S(2)}) collective-permute-start(bf16[160,512]{1,0:T(8,128)(2,1)S(1)} %pass_on.2), channel_id=1, source_target_pairs={{0,2},{1,3},{2,0},{3,1},{4,6},{5,7},{6,4},{7,5},{8,10},{9,11},{10,... | collective-permute-start | bytes 491528 | tf_op jit(solution)/shard_map/ppermute | solution.py:297
  29.3 6.1 %collective-permute-done.11.refs_1_.refs_4_ = bf16[192,512]{1,0:T(8,128)(2,1)S(1)} collective-permute-done((bf16[192,512]{1,0:T(8,128)(2,1)S(1)}, bf16[192,512]{1,0:T(8,128)(2,1)S(1)}, u32[]{:S(2)}, u32[]{:S(2)}) %collective-permute-start.11) | collective-permute-done | bytes 196640 | tf_op jit(solution)/shard_map/ppermute | solution.py:297
  36.1 6.5 %collective-permute-done.12.refs_5_ = bf16[96,512]{1,0:T(8,128)(2,1)S(1)} collective-permute-done((bf16[96,512]{1,0:T(8,128)(2,1)S(1)}, bf16[96,512]{1,0:T(8,128)(2,1)S(1)}, u32[]{:S(2)}, u32[]{:S(2)}) %collective-permute-start.12) | collective-permute-done | bytes 98336 | tf_op jit(solution)/shard_map/ppermute | solution.py:297
  42.6 1.1 %layer.1 = (bf16[512,256]{1,0:T(8,128)(2,1)}, bf16[512,256]{1,0:T(8,128)(2,1)S(1)}, bf16[256,512]{1,0:T(8,128)(2,1)S(1)}, bf16[256,512]{1,0:T(8,128)(2,1)S(1)}, ...) custom-call(s32[1]{0:T(128)} %bitcast.row, bf16[256,256]{1,0:T(8,128)(2,1)S(1)} %copy-done.2, ...), custom_call_target="tpu_custom_call" | custom-call | flops 1 | bytes 1 | tf_op jit(solution)/shard_map/layer/pallas_call | solution.py:261
  43.7 2.2 %collective-permute-start.22 = (bf16[160,512]{1,0:T(8,128)(2,1)S(1)}, bf16[160,512]{1,0:T(8,128)(2,1)S(1)}, u32[]{:S(2)}, u32[]{:S(2)}) collective-permute-start(bf16[160,512]{1,0:T(8,128)(2,1)S(1)} %get-tuple-element.86), channel_id=1, source_target_pairs={{0,2},{1,3},{2,0},{3,1},{4,6},{5,7},{6,4},{7,5},{8,10},{9,11},{10,... | collective-permute-start | bytes 491528 | tf_op jit(solution)/shard_map/ppermute | solution.py:297
  47.6 2.4 %collective-permute-start.16 = (f32[2,32,256]{2,1,0:T(8,128)S(1)}, f32[2,32,256]{2,1,0:T(8,128)S(1)}, u32[]{:S(2)}, u32[]{:S(2)}) collective-permute-start(f32[2,32,256]{2,1,0:T(8,128)S(1)} %get-tuple-element.81), channel_id=1, source_target_pairs={{0,8},{4,12},{8,0},{12,4},{16,24},{20,28},{24,16},{28,20},{1,9},{5... | collective-permute-start | bytes 196616 | tf_op jit(solution)/shard_map/ppermute | solution.py:297
  50.0 2.6 %collective-permute-done.16.refs_1_ = f32[2,32,256]{2,1,0:T(8,128)S(1)} collective-permute-done((f32[2,32,256]{2,1,0:T(8,128)S(1)}, f32[2,32,256]{2,1,0:T(8,128)S(1)}, u32[]{:S(2)}, u32[]{:S(2)}) %collective-permute-start.16) | collective-permute-done | bytes 65568 | tf_op jit(solution)/shard_map/ppermute | solution.py:297
  52.7 1.8 %collective-permute-start.18 = (f32[1,32,256]{2,1,0:T(8,128)S(1)}, f32[1,32,256]{2,1,0:T(8,128)S(1)}, u32[]{:S(2)}, u32[]{:S(2)}) collective-permute-start(f32[1,32,256]{2,1,0:T(8,128)S(1)} %get-tuple-element.85), channel_id=1, source_target_pairs={{0,16},{4,20},{8,24},{12,28},{16,0},{20,4},{24,8},{28,12},{1,17},{... | collective-permute-start | bytes 98312 | tf_op jit(solution)/shard_map/ppermute | solution.py:297
  54.5 2.2 %collective-permute-start.23 = (bf16[160,512]{1,0:T(8,128)(2,1)S(1)}, bf16[160,512]{1,0:T(8,128)(2,1)S(1)}, u32[]{:S(2)}, u32[]{:S(2)}) collective-permute-start(bf16[160,512]{1,0:T(8,128)(2,1)S(1)} %collective-permute-done.22.refs_2_), channel_id=1, source_target_pairs={{0,1},{1,0},{2,3},{3,2},{4,5},{5,4},{6,7},{7,6},{8,9},{9,8},{10,11... | collective-permute-start | bytes 491528 | tf_op jit(solution)/shard_map/ppermute | solution.py:297
  56.6 1.9 %collective-permute-done.13.refs_0_.refs_4_ = bf16[96,512]{1,0:T(8,128)(2,1)S(1)} collective-permute-done((bf16[96,512]{1,0:T(8,128)(2,1)S(1)}, bf16[96,512]{1,0:T(8,128)(2,1)S(1)}, u32[]{:S(2)}, u32[]{:S(2)}) %collective-permute-start.13) | collective-permute-done | bytes 98336 | tf_op jit(solution)/shard_map/ppermute | solution.py:297
  58.7 5.5 %collective-permute-done.19.refs_1_.refs_5_ = bf16[128,512]{1,0:T(8,128)(2,1)S(1)} collective-permute-done((bf16[128,512]{1,0:T(8,128)(2,1)S(1)}, bf16[128,512]{1,0:T(8,128)(2,1)S(1)}, u32[]{:S(2)}, u32[]{:S(2)}) %collective-permute-start.19) | collective-permute-done | bytes 131104 | tf_op jit(solution)/shard_map/ppermute | solution.py:297
  64.2 2.5 %backward_products.1 = (bf16[128,4096]{1,0:T(8,128)(2,1)S(1)}, bf16[32,4096]{1,0:T(8,128)(2,1)S(1)}, bf16[32,4096]{1,0:T(8,128)(2,1)S(1)}, bf16[32,4096]{1,0:T(8,128)(2,1)S(1)}, bf16[32,4096]{1,0:T(8,128)(2,1)S(1)}) custom-call(s32[1]{0:T(128)} %bitcast.1.place, s32[1,1]{1,0:T(1,128)S(6)} %copy.10.count, s32[96]{0:T(128)S(1)} %get-tuple-element.53.rows, ...), custom_call_target="tpu_custom_call" | custom-call | flops 1 | bytes 1 | tf_op jit(solution)/shard_map/backward_products/pallas_call | solution.py:203
  67.9 4.1 %collective-permute-done.20.refs_1_ = f32[32,256]{1,0:T(8,128)S(1)} collective-permute-done((f32[32,256]{1,0:T(8,128)S(1)}, f32[32,256]{1,0:T(8,128)S(1)}, u32[]{:S(2)}, u32[]{:S(2)}) %collective-permute-start.20) | collective-permute-done | bytes 32800 | tf_op jit(solution)/shard_map/ppermute | solution.py:297
  72.1 2.1 %collective-permute-start.25 = (bf16[32,4224]{1,0:T(8,128)(2,1)S(1)}, bf16[32,4224]{1,0:T(8,128)(2,1)S(1)}, u32[]{:S(2)}, u32[]{:S(2)}) collective-permute-start(bf16[32,4224]{1,0:T(8,128)(2,1)S(1)} %far_sums.1), channel_id=1, source_target_pairs={{0,8},{4,20},{8,0},{12,28},{16,24},{20,4},{24,16},{28,12},{1,9},{5... | collective-permute-start | bytes 811016 | tf_op jit(solution)/shard_map/ppermute | solution.py:488
  74.1 2.3 %collective-permute-start.26 = (bf16[32,4096]{1,0:T(8,128)(2,1)S(1)}, bf16[32,4096]{1,0:T(8,128)(2,1)S(1)}, u32[]{:S(2)}, u32[]{:S(2)}) collective-permute-start(bf16[32,4096]{1,0:T(8,128)(2,1)S(1)} %get-tuple-element.92), channel_id=1, source_target_pairs={{0,4},{4,0},{8,12},{12,8},{16,20},{20,16},{24,28},{28,24},{1,5},{5... | collective-permute-start | bytes 786440 | tf_op jit(solution)/shard_map/ppermute | solution.py:297
  76.9 1.4 %collective-permute-done.21.sibling = f32[32,256]{1,0:T(8,128)S(1)} collective-permute-done((f32[32,256]{1,0:T(8,128)S(1)}, f32[32,256]{1,0:T(8,128)S(1)}, u32[]{:S(2)}, u32[]{:S(2)}) %collective-permute-start.21) | collective-permute-done | bytes 32800 | tf_op jit(solution)/shard_map/ppermute | solution.py:297
  79.1 2.1 %collective-permute-start.29 = (bf16[32,4608]{1,0:T(8,128)(2,1)S(1)}, bf16[32,4608]{1,0:T(8,128)(2,1)S(1)}, u32[]{:S(2)}, u32[]{:S(2)}) collective-permute-start(bf16[32,4608]{1,0:T(8,128)(2,1)S(1)} %get-tuple-element.96), channel_id=1, source_target_pairs={{0,8},{4,12},{8,0},{12,4},{16,24},{20,28},{24,16},{28,20},{1,9},{5... | collective-permute-start | bytes 884744 | tf_op jit(solution)/shard_map/ppermute | solution.py:297
  81.2 2.7 %collective-permute-start.30 = (bf16[32,4608]{1,0:T(8,128)(2,1)S(1)}, bf16[32,4608]{1,0:T(8,128)(2,1)S(1)}, u32[]{:S(2)}, u32[]{:S(2)}) collective-permute-start(bf16[32,4608]{1,0:T(8,128)(2,1)S(1)} %get-tuple-element.97), channel_id=1, source_target_pairs={{0,16},{4,20},{8,24},{12,28},{16,0},{20,4},{24,8},{28,12},{1,17},{... | collective-permute-start | bytes 884744 | tf_op jit(solution)/shard_map/ppermute | solution.py:297
  83.9 1.4 %collective-permute-start.31 = (bf16[32,512]{1,0:T(8,128)(2,1)S(1)}, bf16[32,512]{1,0:T(8,128)(2,1)S(1)}, u32[]{:S(2)}, u32[]{:S(2)}) collective-permute-start(bf16[32,512]{1,0:T(8,128)(2,1)S(1)} %get-tuple-element.98.refs_3_), channel_id=1, source_target_pairs={{0,24},{4,28},{8,16},{12,20},{16,8},{20,12},{24,0},{28,4},{1,25},{... | collective-permute-start | bytes 98312 | tf_op jit(solution)/shard_map/ppermute | solution.py:297
  85.3 6.7 %collective-permute-done.31.refs_4_ = bf16[32,512]{1,0:T(8,128)(2,1)S(1)} collective-permute-done((bf16[32,512]{1,0:T(8,128)(2,1)S(1)}, bf16[32,512]{1,0:T(8,128)(2,1)S(1)}, u32[]{:S(2)}, u32[]{:S(2)}) %collective-permute-start.31) | collective-permute-done | bytes 32800 | tf_op jit(solution)/shard_map/ppermute | solution.py:297
  (55 shorter events, 9.1 us)
Async XLA Ops:
  0.6 9.5 %collective-permute-start.3 = (bf16[32,4096]{1,0:T(8,128)(2,1)}, bf16[32,4096]{1,0:T(8,128)(2,1)S(1)}, u32[]{:S(2)}, u32[]{:S(2)}) collective-permute-start(bf16[32,4096]{1,0:T(8,128)(2,1)} %bitcast.7), channel_id=1, source_target_pairs={{0,16},{4,20},{8,24},{12,28},{16,0},{20,4},{24,8},{28,12},{1,17},{... | collective-permute-start | bytes 786440 | tf_op jit(solution)/shard_map/ppermute | solution.py:297
  3.7 8.0 %collective-permute-start.1 = (bf16[32,4096]{1,0:T(8,128)(2,1)}, bf16[32,4096]{1,0:T(8,128)(2,1)S(1)}, u32[]{:S(2)}, u32[]{:S(2)}) collective-permute-start(bf16[32,4096]{1,0:T(8,128)(2,1)} %bitcast.8), channel_id=1, source_target_pairs={{0,8},{4,12},{8,0},{12,4},{16,24},{20,28},{24,16},{28,20},{1,9},{5... | collective-permute-start | bytes 786440 | tf_op jit(solution)/shard_map/ppermute | solution.py:297
  5.2 9.9 %collective-permute-start = (bf16[32,4096]{1,0:T(8,128)(2,1)}, bf16[32,4096]{1,0:T(8,128)(2,1)S(1)}, u32[]{:S(2)}, u32[]{:S(2)}) collective-permute-start(bf16[32,4096]{1,0:T(8,128)(2,1)} %bitcast.9), channel_id=1, source_target_pairs={{0,4},{4,0},{8,12},{12,8},{16,20},{20,16},{24,28},{28,24},{1,5},{5... | collective-permute-start | bytes 786440 | tf_op jit(solution)/shard_map/ppermute | solution.py:297
  11.7 3.4 %collective-permute-start.2 = (bf16[32,4096]{1,0:T(8,128)(2,1)S(1)}, bf16[32,4096]{1,0:T(8,128)(2,1)S(1)}, u32[]{:S(2)}, u32[]{:S(2)}) collective-permute-start(bf16[32,4096]{1,0:T(8,128)(2,1)S(1)} %collective-permute-done.1.refs_2_), channel_id=1, source_target_pairs={{0,4},{4,0},{8,12},{12,8},{16,20},{20,16},{24,28},{28,24},{1,5},{5... | collective-permute-start | bytes 786440 | tf_op jit(solution)/shard_map/ppermute | solution.py:297
  11.7 3.4 %collective-permute-start.4 = (bf16[32,4096]{1,0:T(8,128)(2,1)S(1)}, bf16[32,4096]{1,0:T(8,128)(2,1)S(1)}, u32[]{:S(2)}, u32[]{:S(2)}) collective-permute-start(bf16[32,4096]{1,0:T(8,128)(2,1)S(1)} %collective-permute-done.3.refs_4_), channel_id=1, source_target_pairs={{0,4},{4,0},{8,12},{12,8},{16,20},{20,16},{24,28},{28,24},{1,5},{5... | collective-permute-start | bytes 786440 | tf_op jit(solution)/shard_map/ppermute | solution.py:297
  12.2 7.3 %collective-permute-start.7 = (bf16[16,4096]{1,0:T(8,128)(2,1)S(1)}, bf16[16,4096]{1,0:T(8,128)(2,1)S(1)}, u32[]{:S(2)}, u32[]{:S(2)}) collective-permute-start(bf16[16,4096]{1,0:T(8,128)(2,1)S(1)} %get-tuple-element.62), channel_id=1, source_target_pairs={{0,24},{4,28},{8,16},{12,20},{16,8},{20,12},{24,0},{28,4},{1,25},{... | collective-permute-start | bytes 393224 | tf_op jit(solution)/shard_map/ppermute | solution.py:297
  13.6 7.7 %collective-permute-start.6 = (bf16[16,4096]{1,0:T(8,128)(2,1)S(1)}, bf16[16,4096]{1,0:T(8,128)(2,1)S(1)}, u32[]{:S(2)}, u32[]{:S(2)}) collective-permute-start(bf16[16,4096]{1,0:T(8,128)(2,1)S(1)} %get-tuple-element.60), channel_id=1, source_target_pairs={{0,24},{4,28},{8,16},{12,20},{16,8},{20,12},{24,0},{28,4},{1,25},{... | collective-permute-start | bytes 393224 | tf_op jit(solution)/shard_map/ppermute | solution.py:297
  17.4 9.1 %collective-permute-start.5 = (bf16[320,512]{1,0:T(8,128)(2,1)S(1)}, bf16[320,512]{1,0:T(8,128)(2,1)S(1)}, u32[]{:S(2)}, u32[]{:S(2)}) collective-permute-start(bf16[320,512]{1,0:T(8,128)(2,1)S(1)} %get-tuple-element.59), channel_id=1, source_target_pairs={{0,1},{1,0},{2,3},{3,2},{4,5},{5,4},{6,7},{7,6},{8,9},{9,8},{10,11... | collective-permute-start | bytes 983048 | tf_op jit(solution)/shard_map/ppermute | solution.py:297
  21.3 1.3 %collective-permute-start.8 = (bf16[16,4096]{1,0:T(8,128)(2,1)S(1)}, bf16[16,4096]{1,0:T(8,128)(2,1)S(1)}, u32[]{:S(2)}, u32[]{:S(2)}) collective-permute-start(bf16[16,4096]{1,0:T(8,128)(2,1)S(1)} %collective-permute-done.6.refs_0_), channel_id=1, source_target_pairs={{0,4},{4,0},{8,12},{12,8},{16,20},{20,16},{24,28},{28,24},{1,5},{5... | collective-permute-start | bytes 393224 | tf_op jit(solution)/shard_map/ppermute | solution.py:297
  21.3 1.5 %collective-permute-start.9 = (bf16[16,4096]{1,0:T(8,128)(2,1)S(1)}, bf16[16,4096]{1,0:T(8,128)(2,1)S(1)}, u32[]{:S(2)}, u32[]{:S(2)}) collective-permute-start(bf16[16,4096]{1,0:T(8,128)(2,1)S(1)} %collective-permute-done.7.refs_1_), channel_id=1, source_target_pairs={{0,4},{4,0},{8,12},{12,8},{16,20},{20,16},{24,28},{28,24},{1,5},{5... | collective-permute-start | bytes 393224 | tf_op jit(solution)/shard_map/ppermute | solution.py:297
  24.7 10.7 %collective-permute-start.11 = (bf16[192,512]{1,0:T(8,128)(2,1)S(1)}, bf16[192,512]{1,0:T(8,128)(2,1)S(1)}, u32[]{:S(2)}, u32[]{:S(2)}) collective-permute-start(bf16[192,512]{1,0:T(8,128)(2,1)S(1)} %get-tuple-element.70), channel_id=1, source_target_pairs={{0,1},{1,0},{2,3},{3,2},{4,5},{5,4},{6,7},{7,6},{8,9},{9,8},{10,11... | collective-permute-start | bytes 589832 | tf_op jit(solution)/shard_map/ppermute | solution.py:297
  26.6 16.0 %collective-permute-start.10 = (bf16[160,512]{1,0:T(8,128)(2,1)S(1)}, bf16[160,512]{1,0:T(8,128)(2,1)S(1)}, u32[]{:S(2)}, u32[]{:S(2)}) collective-permute-start(bf16[160,512]{1,0:T(8,128)(2,1)S(1)} %pass_on.2), channel_id=1, source_target_pairs={{0,2},{1,3},{2,0},{3,1},{4,6},{5,7},{6,4},{7,5},{8,10},{9,11},{10,... | collective-permute-start | bytes 491528 | tf_op jit(solution)/shard_map/ppermute | solution.py:297
  35.4 7.1 %collective-permute-start.12 = (bf16[96,512]{1,0:T(8,128)(2,1)S(1)}, bf16[96,512]{1,0:T(8,128)(2,1)S(1)}, u32[]{:S(2)}, u32[]{:S(2)}) collective-permute-start(bf16[96,512]{1,0:T(8,128)(2,1)S(1)} %pass_on.3), channel_id=1, source_target_pairs={{0,2},{1,3},{2,0},{3,1},{4,6},{5,7},{6,4},{7,5},{8,10},{9,11},{10,... | collective-permute-start | bytes 294920 | tf_op jit(solution)/shard_map/ppermute | solution.py:297
  43.7 14.9 %collective-permute-start.17 = (bf16[256,512]{1,0:T(8,128)(2,1)S(1)}, bf16[256,512]{1,0:T(8,128)(2,1)S(1)}, u32[]{:S(2)}, u32[]{:S(2)}) collective-permute-start(bf16[256,512]{1,0:T(8,128)(2,1)S(1)} %get-tuple-element.83.refs_0_), channel_id=1, source_target_pairs={{0,1},{1,0},{2,3},{3,2},{4,5},{5,4},{6,7},{7,6},{8,9},{9,8},{10,11... | collective-permute-start | bytes 786440 | tf_op jit(solution)/shard_map/ppermute | solution.py:297
  43.7 10.8 %collective-permute-start.22 = (bf16[160,512]{1,0:T(8,128)(2,1)S(1)}, bf16[160,512]{1,0:T(8,128)(2,1)S(1)}, u32[]{:S(2)}, u32[]{:S(2)}) collective-permute-start(bf16[160,512]{1,0:T(8,128)(2,1)S(1)} %get-tuple-element.86), channel_id=1, source_target_pairs={{0,2},{1,3},{2,0},{3,1},{4,6},{5,7},{6,4},{7,5},{8,10},{9,11},{10,... | collective-permute-start | bytes 491528 | tf_op jit(solution)/shard_map/ppermute | solution.py:297
  46.1 1.3 %collective-permute-start.14 = (f32[2,32,256]{2,1,0:T(8,128)S(1)}, f32[2,32,256]{2,1,0:T(8,128)S(1)}, u32[]{:S(2)}, u32[]{:S(2)}) collective-permute-start(f32[2,32,256]{2,1,0:T(8,128)S(1)} %get-tuple-element.78), channel_id=1, source_target_pairs={{0,4},{4,0},{8,12},{12,8},{16,20},{20,16},{24,28},{28,24},{1,5},{5... | collective-permute-start | bytes 196616 | tf_op jit(solution)/shard_map/ppermute | solution.py:297
  46.2 1.4 %collective-permute-start.15 = (f32[2,32,256]{2,1,0:T(8,128)S(1)}, f32[2,32,256]{2,1,0:T(8,128)S(1)}, u32[]{:S(2)}, u32[]{:S(2)}) collective-permute-start(f32[2,32,256]{2,1,0:T(8,128)S(1)} %get-tuple-element.79), channel_id=1, source_target_pairs={{0,4},{4,0},{8,12},{12,8},{16,20},{20,16},{24,28},{28,24},{1,5},{5... | collective-permute-start | bytes 196616 | tf_op jit(solution)/shard_map/ppermute | solution.py:297
  46.7 11.9 %collective-permute-start.13 = (bf16[96,512]{1,0:T(8,128)(2,1)S(1)}, bf16[96,512]{1,0:T(8,128)(2,1)S(1)}, u32[]{:S(2)}, u32[]{:S(2)}) collective-permute-start(bf16[96,512]{1,0:T(8,128)(2,1)S(1)} %get-tuple-element.74), channel_id=1, source_target_pairs={{0,2},{1,3},{2,0},{3,1},{4,6},{5,7},{6,4},{7,5},{8,10},{9,11},{10,... | collective-permute-start | bytes 294920 | tf_op jit(solution)/shard_map/ppermute | solution.py:297
  47.6 5.0 %collective-permute-start.16 = (f32[2,32,256]{2,1,0:T(8,128)S(1)}, f32[2,32,256]{2,1,0:T(8,128)S(1)}, u32[]{:S(2)}, u32[]{:S(2)}) collective-permute-start(f32[2,32,256]{2,1,0:T(8,128)S(1)} %get-tuple-element.81), channel_id=1, source_target_pairs={{0,8},{4,12},{8,0},{12,4},{16,24},{20,28},{24,16},{28,20},{1,9},{5... | collective-permute-start | bytes 196616 | tf_op jit(solution)/shard_map/ppermute | solution.py:297
  52.7 5.9 %collective-permute-start.18 = (f32[1,32,256]{2,1,0:T(8,128)S(1)}, f32[1,32,256]{2,1,0:T(8,128)S(1)}, u32[]{:S(2)}, u32[]{:S(2)}) collective-permute-start(f32[1,32,256]{2,1,0:T(8,128)S(1)} %get-tuple-element.85), channel_id=1, source_target_pairs={{0,16},{4,20},{8,24},{12,28},{16,0},{20,4},{24,8},{28,12},{1,17},{... | collective-permute-start | bytes 98312 | tf_op jit(solution)/shard_map/ppermute | solution.py:297
  54.5 9.7 %collective-permute-start.23 = (bf16[160,512]{1,0:T(8,128)(2,1)S(1)}, bf16[160,512]{1,0:T(8,128)(2,1)S(1)}, u32[]{:S(2)}, u32[]{:S(2)}) collective-permute-start(bf16[160,512]{1,0:T(8,128)(2,1)S(1)} %collective-permute-done.22.refs_2_), channel_id=1, source_target_pairs={{0,1},{1,0},{2,3},{3,2},{4,5},{5,4},{6,7},{7,6},{8,9},{9,8},{10,11... | collective-permute-start | bytes 491528 | tf_op jit(solution)/shard_map/ppermute | solution.py:297
  58.6 5.6 %collective-permute-start.19 = (bf16[128,512]{1,0:T(8,128)(2,1)S(1)}, bf16[128,512]{1,0:T(8,128)(2,1)S(1)}, u32[]{:S(2)}, u32[]{:S(2)}) collective-permute-start(bf16[128,512]{1,0:T(8,128)(2,1)S(1)} %with_chunk.1.refs_0_), channel_id=1, source_target_pairs={{0,1},{1,0},{2,3},{3,2},{4,5},{5,4},{6,7},{7,6},{8,9},{9,8},{10,11... | collective-permute-start | bytes 393224 | tf_op jit(solution)/shard_map/ppermute | solution.py:297
  66.8 5.2 %collective-permute-start.24 = (bf16[32,4096]{1,0:T(8,128)(2,1)S(1)}, bf16[32,4096]{1,0:T(8,128)(2,1)S(1)}, u32[]{:S(2)}, u32[]{:S(2)}) collective-permute-start(bf16[32,4096]{1,0:T(8,128)(2,1)S(1)} %get-tuple-element.91), channel_id=1, source_target_pairs={{0,4},{4,0},{8,12},{12,8},{16,20},{20,16},{24,28},{28,24},{1,5},{5... | collective-permute-start | bytes 786440 | tf_op jit(solution)/shard_map/ppermute | solution.py:297
  66.8 5.1 %collective-permute-start.20 = (f32[32,256]{1,0:T(8,128)S(1)}, f32[32,256]{1,0:T(8,128)S(1)}, u32[]{:S(2)}, u32[]{:S(2)}) collective-permute-start(f32[32,256]{1,0:T(8,128)S(1)} %chunk_sum.2.refs_0_), channel_id=1, source_target_pairs={{0,2},{1,3},{2,0},{3,1},{4,6},{5,7},{6,4},{7,5},{8,10},{9,11},{10,... | collective-permute-start | bytes 98312 | tf_op jit(solution)/shard_map/ppermute | solution.py:297
  72.1 6.5 %collective-permute-start.25 = (bf16[32,4224]{1,0:T(8,128)(2,1)S(1)}, bf16[32,4224]{1,0:T(8,128)(2,1)S(1)}, u32[]{:S(2)}, u32[]{:S(2)}) collective-permute-start(bf16[32,4224]{1,0:T(8,128)(2,1)S(1)} %far_sums.1), channel_id=1, source_target_pairs={{0,8},{4,20},{8,0},{12,28},{16,24},{20,4},{24,16},{28,12},{1,9},{5... | collective-permute-start | bytes 811016 | tf_op jit(solution)/shard_map/ppermute | solution.py:488
  74.1 4.2 %collective-permute-start.26 = (bf16[32,4096]{1,0:T(8,128)(2,1)S(1)}, bf16[32,4096]{1,0:T(8,128)(2,1)S(1)}, u32[]{:S(2)}, u32[]{:S(2)}) collective-permute-start(bf16[32,4096]{1,0:T(8,128)(2,1)S(1)} %get-tuple-element.92), channel_id=1, source_target_pairs={{0,4},{4,0},{8,12},{12,8},{16,20},{20,16},{24,28},{28,24},{1,5},{5... | collective-permute-start | bytes 786440 | tf_op jit(solution)/shard_map/ppermute | solution.py:297
  76.4 2.0 %collective-permute-start.27 = (bf16[32,4096]{1,0:T(8,128)(2,1)S(1)}, bf16[32,4096]{1,0:T(8,128)(2,1)S(1)}, u32[]{:S(2)}, u32[]{:S(2)}) collective-permute-start(bf16[32,4096]{1,0:T(8,128)(2,1)S(1)} %get-tuple-element.93), channel_id=1, source_target_pairs={{0,4},{4,0},{8,12},{12,8},{16,20},{20,16},{24,28},{28,24},{1,5},{5... | collective-permute-start | bytes 786440 | tf_op jit(solution)/shard_map/ppermute | solution.py:297
  76.4 2.0 %collective-permute-start.28 = (bf16[32,4096]{1,0:T(8,128)(2,1)S(1)}, bf16[32,4096]{1,0:T(8,128)(2,1)S(1)}, u32[]{:S(2)}, u32[]{:S(2)}) collective-permute-start(bf16[32,4096]{1,0:T(8,128)(2,1)S(1)} %get-tuple-element.94), channel_id=1, source_target_pairs={{0,4},{4,0},{8,12},{12,8},{16,20},{20,16},{24,28},{28,24},{1,5},{5... | collective-permute-start | bytes 786440 | tf_op jit(solution)/shard_map/ppermute | solution.py:297
  76.9 1.4 %collective-permute-start.21 = (f32[32,256]{1,0:T(8,128)S(1)}, f32[32,256]{1,0:T(8,128)S(1)}, u32[]{:S(2)}, u32[]{:S(2)}) collective-permute-start(f32[32,256]{1,0:T(8,128)S(1)} %chunk_sum.3.chunk), channel_id=1, source_target_pairs={{0,4},{4,0},{8,12},{12,8},{16,20},{20,16},{24,28},{28,24},{1,5},{5... | collective-permute-start | bytes 98312 | tf_op jit(solution)/shard_map/ppermute | solution.py:297
  79.1 12.8 %collective-permute-start.29 = (bf16[32,4608]{1,0:T(8,128)(2,1)S(1)}, bf16[32,4608]{1,0:T(8,128)(2,1)S(1)}, u32[]{:S(2)}, u32[]{:S(2)}) collective-permute-start(bf16[32,4608]{1,0:T(8,128)(2,1)S(1)} %get-tuple-element.96), channel_id=1, source_target_pairs={{0,8},{4,12},{8,0},{12,4},{16,24},{20,28},{24,16},{28,20},{1,9},{5... | collective-permute-start | bytes 884744 | tf_op jit(solution)/shard_map/ppermute | solution.py:297
  81.2 10.8 %collective-permute-start.30 = (bf16[32,4608]{1,0:T(8,128)(2,1)S(1)}, bf16[32,4608]{1,0:T(8,128)(2,1)S(1)}, u32[]{:S(2)}, u32[]{:S(2)}) collective-permute-start(bf16[32,4608]{1,0:T(8,128)(2,1)S(1)} %get-tuple-element.97), channel_id=1, source_target_pairs={{0,16},{4,20},{8,24},{12,28},{16,0},{20,4},{24,8},{28,12},{1,17},{... | collective-permute-start | bytes 884744 | tf_op jit(solution)/shard_map/ppermute | solution.py:297
  83.9 8.1 %collective-permute-start.31 = (bf16[32,512]{1,0:T(8,128)(2,1)S(1)}, bf16[32,512]{1,0:T(8,128)(2,1)S(1)}, u32[]{:S(2)}, u32[]{:S(2)}) collective-permute-start(bf16[32,512]{1,0:T(8,128)(2,1)S(1)} %get-tuple-element.98.refs_3_), channel_id=1, source_target_pairs={{0,24},{4,28},{8,16},{12,20},{16,8},{20,12},{24,0},{28,4},{1,25},{... | collective-permute-start | bytes 98312 | tf_op jit(solution)/shard_map/ppermute | solution.py:297
  (3 other events, 64.8 us)
